TPU v7x, 512 devices: a whole 4x4x16 slice. The times are simulated.
512 devices in a mesh: ops: 32 (over x, z_hi, core), sec: 16 (over z_lo, y).
Axes of the slice: x: 4, y: 4, z: 16 (z_hi: 4, z_lo: 4; z = z_hi * 4 + z_lo), core: 2. Of those that a mesh axis runs over, the one named last changes fastest.
Arguments:
- wave_t: bfloat16 [16, 512, 512], P(None, 'sec'), may hold values from -6 to 6
- left_ops: bfloat16 [96, 512, 512], P('ops'), may hold values from -0.25 to 0.25
- right_ops: bfloat16 [96, 512, 512], P('ops'), may hold values from -0.02734375 to 0.02734375
- pattern: int32 [96, 16], P('ops'), may hold values from 0 to 15
- sector_size: int32 [16], replicated, may hold values from 128 to 512, as said below
Outputs:
- first_image: bfloat16 [16, 512, 512], P(None, 'sec')
- second_image: bfloat16 [16, 512, 512], P(None, 'sec')
Inputs may be any that keep to these rules, and one draw needn't show every extreme that they name: `sector_size`: multiples of 128; the largest is exactly 512 and the smallest exactly 128.
All inputs are finite; a program needn't handle non-finite values.
Results may differ from a plain program's by a relative error of at most 0.009.
Values may be sent and summed in bfloat16 or wider, within the bound.
A program may use at most 64 MiB of HBM per device.

v0:
```python
import jax
import jax.numpy as jnp
from jax import lax
from jax.sharding import PartitionSpec as P


def select_sources(left_all, pattern):
    return jnp.take_along_axis(left_all, pattern[:, :, None, None], axis=1)


def on_device(wave_t, left_ops, right_ops, pattern, sector_size):
    sec_count = lax.axis_size("sec")
    sec_place = lax.axis_index("sec")
    order = left_ops.shape[1]
    width = order // sec_count
    inside = jnp.arange(order)[None, :] < sector_size[:, None]
    local_inside = lax.dynamic_slice_in_dim(inside, sec_place * width, width, 1)
    slab_keep = local_inside[:, :, None] & inside[:, None, :]
    zero = jnp.zeros((), jnp.bfloat16)
    columns_t = jnp.where(slab_keep, wave_t, zero)
    rows_left = lax.dynamic_slice_in_dim(left_ops, sec_place * width, width, 1)

    def combine_terms(partial_rows):
        partial_rows = jnp.where(slab_keep, partial_rows, jnp.zeros((), jnp.float32))
        summed = lax.psum(partial_rows, "ops")
        return summed.astype(jnp.bfloat16)

    full_wave = lax.all_gather(columns_t, "sec", axis=1, tiled=True)
    left_all = jnp.einsum("tij,bcj->tbic", rows_left, full_wave, preferred_element_type=jnp.float32)
    left_rows = select_sources(left_all.astype(jnp.bfloat16), pattern)
    first_partial = jnp.einsum(
        "tbic,tjc->bij", left_rows, right_ops, preferred_element_type=jnp.float32
    )
    first_image = combine_terms(first_partial)
    full_image = lax.all_gather(first_image, "sec", axis=1, tiled=True)
    left_all = jnp.einsum(
        "tij,bjc->tbic", rows_left, full_image, preferred_element_type=jnp.float32
    )
    left_rows = select_sources(left_all.astype(jnp.bfloat16), pattern)
    second_partial = jnp.einsum(
        "tbic,tjc->bij", left_rows, right_ops, preferred_element_type=jnp.float32
    )
    second_image = combine_terms(second_partial)
    return (first_image, second_image)


def solution(mesh):
    return jax.shard_map(
        on_device,
        mesh=mesh,
        in_specs=(
            P(None, "sec", None),
            P("ops", None, None),
            P("ops", None, None),
            P("ops", None),
            P(),
        ),
        out_specs=(P(None, "sec", None), P(None, "sec", None)),
        check_vma=False,
    )
```

profile of v0, /device:TPU:1, one launch (start us, length us, event | category | flops | bytes accessed | tf_op | source)
XLA Modules:
  0.0 615.5 jit_solution(9468254537588516526)
XLA Ops:
  7.2 0.0 copy-start
  7.2 0.0 copy-start.1
  7.2 0.0 all-gather.3.cloned.1.call-start
  7.2 0.8 iota_compare_fusion
  8.1 0.1 constant_dynamic-slice_fusion
  8.2 2.1 and_select_fusion.2
  10.3 0.0 all-gather.3.cloned.1.call-update
  10.3 0.0 all-gather.5.cloned.1.call-start
  10.3 0.0 copy-done.1
  10.4 0.1 copy.11
  10.5 0.1 reshape.63
  10.6 113.1 %all-gather.3.cloned.1.call-done = bf16[16,512,512]{2,1,0:T(8,128)(2,1)} async-done(((bf16[16,32,512]{2,1,0:T(8,128)(2,1)}), bf16[16,512,512]{2,1,0:T(8,128)(2,1)}) %all-gather.3.cloned.1.call-update) | async-done | bytes 8388624 | tf_op jit(solution)/shard_map/all_gather | solution.py:28
  123.6 0.0 copy-done
  123.6 6.0 fusion.19
  129.7 2.0 gather_fusion
  131.7 2.9 and_select_fusion.1
  134.6 179.9 %all-reduce.2 = bf16[16,32,512]{2,1,0:T(8,128)(2,1)} all-reduce(f32[16,32,512]{2,1,0:T(8,128)S(1)} %and_select_fusion.1), channel_id=1, replica_groups=mesh['ops'=32,'sec'=16] {'ops'}, use_global_device_ids=true, to_apply=%region_0.0 | all-reduce | flops 262144 | bytes 1572864 | tf_op jit(solution)/shard_map/psum | solution.py:25
  314.5 0.0 all-gather.5.cloned.1.call-update
  314.5 105.1 %all-gather.5.cloned.1.call-done = bf16[16,512,512]{2,1,0:T(8,128)(2,1)} async-done(((bf16[16,32,512]{2,1,0:T(8,128)(2,1)}), bf16[16,512,512]{2,1,0:T(8,128)(2,1)}) %all-gather.5.cloned.1.call-update) | async-done | bytes 8388624 | tf_op jit(solution)/shard_map/all_gather | solution.py:35
  419.6 4.9 fusion.16
  424.5 2.0 gather_fusion.1
  426.5 2.9 and_select_fusion
  429.4 179.3 %all-reduce.3 = bf16[16,32,512]{2,1,0:T(8,128)(2,1)} all-reduce(f32[16,32,512]{2,1,0:T(8,128)S(1)} %and_select_fusion), channel_id=1, replica_groups=mesh['ops'=32,'sec'=16] {'ops'}, use_global_device_ids=true, to_apply=%region_1.3 | all-reduce | flops 262144 | bytes 1572864 | tf_op jit(solution)/shard_map/psum | solution.py:25
  (3 shorter events, 0.0 us)
Async XLA Ops:
  7.2 116.5 %copy-start = (bf16[3,512,512]{2,1,0:T(8,128)(2,1)S(1)}, bf16[3,512,512]{2,1,0:T(8,128)(2,1)}, u32[]{:S(2)}) copy-start(bf16[3,512,512]{2,1,0:T(8,128)(2,1)} %param.8) | copy-start | bytes 4718596
  7.2 3.2 copy-start.1
  7.2 116.4 %all-gather.3.cloned.1.call-start = ((), (), s32[]{:S(2)}) async-start(), calls=%async_computation | async-start | bytes 8912896 | tf_op jit(solution)/shard_map/all_gather | solution.py:28
  10.3 409.3 %all-gather.5.cloned.1.call-start = ((), (), s32[]{:S(2)}) async-start(), calls=%async_computation.1 | async-start | bytes 8912896 | tf_op jit(solution)/shard_map/all_gather | solution.py:35
Sparse Core Ops, SparseCore 0:
  10.7 112.9 all-gather.2
  314.6 104.9 all-gather.4
where the time goes:
time: 625 us; the launch traced here: 615 us
  blocking collectives  359 us (57%)
  waiting for transfers between devices  218 us (35%)
  matrix products  16.7 us (3%)
  between operations  14.1 us (2%)
    psum x2, blocking collectives, combine_terms(): summed = lax.psum(partial_rows, 'ops')  359 us
    all_gather x1, waiting for transfers between devices, on_device(): full_wave = lax.all_gather(columns_t, 'sec', axis=1, tiled=True)  113 us
    all_gather x1, waiting for transfers between devices, on_device(): full_image = lax.all_gather(first_image, 'sec', axis=1, tiled=True)  105 us
  transfers between devices with their start and end apart: 2, of which 2 were waited for; matrix products, arithmetic and copies ran while one was open for 0% of the time, Pallas kernels for 0%

commit v1 on v0

v1 whole, which is shorter than its diff:
```python
import jax
import jax.numpy as jnp
from jax import lax
from jax.experimental import pallas as pl
from jax.experimental.pallas import tpu as pltpu
from jax.sharding import PartitionSpec as P

MESH = pl.DeviceIdType.MESH
BF = jnp.bfloat16
F32 = jnp.float32
NT = (((1,), (1,)), ((), ()))
NN = (((1,), (0,)), ((), ()))


def dot(a, b, dims):
    return lax.dot_general(a, b, dims, preferred_element_type=F32)


def kernel(
    wave, lops, rops, pat, sizes, out1, out2,
    wbuf, lf, rf, rsel, lsel, va, vb, mid,
    s0s1, s0r1, s01, r1y1, r1x1, t11, t21, r2x1, r2y1, wf1, wb1, r31, f1,
    s0s2, s0r2, s02, r1y2, r1x2, t12, t22, r2x2, r2y2, wf2, wb2, r32, f2,
    obuf, lsem, ssem, rsem,
):
    ops, sec = lax.axis_index("ops"), lax.axis_index("sec")
    x, zh, c = ops // 8, (ops // 2) % 4, ops % 2
    zl, y = sec // 4, sec % 4
    z = zh * 4 + zl

    def to_x(d):
        return {"ops": ((x + d) % 4 * 4 + zh) * 2 + c, "sec": sec}

    def to_y(d):
        return {"ops": ops, "sec": zl * 4 + (y + d) % 4}

    def to_z(d):
        w = (z + d + 16) % 16
        return {"ops": (x * 4 + w // 4) * 2 + c, "sec": w % 4 * 4 + y}

    def to_zz(dh, dl):
        return {"ops": (x * 4 + (zh + dh) % 4) * 2 + c, "sec": (zl + dl) % 4 * 4 + y}

    other = {"ops": ops + 1 - 2 * c, "sec": sec}

    sent = []
    count = [0]

    def copies(n):
        first = count[0]
        count[0] += n
        return first

    def send(src, dst, index, device):
        cp = pltpu.make_async_remote_copy(
            src_ref=src, dst_ref=dst, send_sem=ssem.at[index], recv_sem=rsem.at[index],
            device_id=device, device_id_type=MESH,
        )
        cp.start()
        sent.append(cp)

    def arrived(ref, index):
        pltpu.make_async_copy(ref, ref, rsem.at[index]).wait()

    load_w = pltpu.make_async_copy(wave, wbuf, lsem.at[0])
    load_r = pltpu.make_async_copy(rops, rf, lsem.at[1])
    load_l = pltpu.make_async_copy(lops, lf, lsem.at[2])
    load_w.start()
    load_r.start()
    load_l.start()
    partners = [other] + [to_y(d) for d in (1, 2, 3)] + [to_x(d) for d in (1, 2, 3)] + [to_z(d) for d in range(1, 16)]
    barrier = pltpu.get_barrier_semaphore()
    for device in partners:
        pl.semaphore_signal(barrier, inc=1, device_id=device, device_id_type=MESH)

    load_w.wait()
    row = lax.broadcasted_iota(jnp.int32, (4, 16, 512), 0) % 2 * 16 + lax.broadcasted_iota(jnp.int32, (4, 16, 512), 1)
    row = row + (zl * 128 + y * 32)
    col = lax.broadcasted_iota(jnp.int32, (4, 16, 512), 2)
    part = lax.broadcasted_iota(jnp.int32, (4, 16, 512), 0) // 2
    edge = jnp.maximum(row, col)

    def mask_wave(k, carry):
        cc, xx = k // 4, k % 4
        size = jnp.where(part == 0, sizes[2 * k], sizes[2 * k + 1])
        va[zl, cc, xx] = jnp.where(edge < size, wbuf[cc, xx].astype(F32), 0.0).astype(BF)
        return carry

    lax.fori_loop(0, 8, mask_wave, 0)
    pl.semaphore_wait(barrier, len(partners))

    z_of = [zl, (zl + 3) % 4, (zl + 1) % 4, (zl + 2) % 4]


    def gather(v, whole_slab):
        a1, b1, a2, b2, cx = copies(4), copies(3), copies(12), copies(16), copies(4)
        mine = v.at[zl, c, x]
        low = mine.at[pl.ds(0, 2)]
        send(low, low, a1, to_z(1))
        send(low, low, a1 + 1, to_z(-1))
        send(mine.at[0], mine.at[0], a1 + 2, to_z(2))
        send(mine.at[1], mine.at[1], a1 + 3, to_z(-2))

        def b2_send(xx, k):
            high = v.at[zl, c, xx, pl.ds(2, 2)]
            send(high, high, b2 + 4 * k, to_z(1))
            send(high, high, b2 + 4 * k + 1, to_z(-1))
            send(v.at[zl, c, xx, 2], v.at[zl, c, xx, 2], b2 + 4 * k + 2, to_z(2))
            send(v.at[zl, c, xx, 3], v.at[zl, c, xx, 3], b2 + 4 * k + 3, to_z(-2))

        def a2_send(k):
            block = v.at[z_of[k], c, x, pl.ds(0, 2)]
            for d in (1, 2, 3):
                send(block, block, a2 + 3 * k + d - 1, to_x(d))

        def a1_wait(k):
            block = v.at[z_of[k], c, x]
            if k < 3:
                arrived(block.at[pl.ds(0, 2)], a1 + k - 1)
            else:
                arrived(block.at[0], a1 + 2)
                arrived(block.at[1], a1 + 3)

        x_of = [x, (x + 3) % 4, (x + 1) % 4, (x + 2) % 4]
        step = [0, 1, 3, 2]
        if whole_slab:
            for k in range(4):
                b2_send(x_of[k], k)
        else:
            high = mine.at[pl.ds(2, 2)]
            for d in (1, 2, 3):
                send(high, high, b1 + d - 1, to_x(d))
            a2_send(0)
            b2_send(x, 0)
        for k in (1, 2, 3):
            if not whole_slab:
                arrived(v.at[zl, c, x_of[k], pl.ds(2, 2)], b1 + step[k] - 1)
                b2_send(x_of[k], k)
            a1_wait(k)
            a2_send(k)
        for k in range(4):
            if k == 0 and whole_slab:
                continue
            for m in (1, 2, 3):
                arrived(v.at[z_of[k], c, x_of[m], pl.ds(0, 2)], a2 + 3 * k + step[m] - 1)
            if k > 0:
                for m in range(4):
                    block = v.at[z_of[k], c, x_of[m]]
                    if k < 3:
                        arrived(block.at[pl.ds(2, 2)], b2 + 4 * m + k - 1)
                    else:
                        arrived(block.at[2], b2 + 4 * m + 2)
                        arrived(block.at[3], b2 + 4 * m + 3)
            send(v.at[z_of[k], c], v.at[z_of[k], c], cx + k, other)

        def other_core():
            for k in range(4):
                if k == 0 and whole_slab:
                    continue
                arrived(v.at[z_of[k], 1 - c], cx + k)

        return other_core

    def reduce(pair, tr, tc, s0s, s0r, s0, r1y, r1x, t1, t2, r2x, r2y, wf, wb, r3):
        p0, py, px, qx, qy, p3 = copies(4), copies(12), copies(3), copies(3), copies(3), copies(3)
        for k, d in enumerate((1, 2, 3, 0)):
            xx = (x + d) % 4
            s0s[xx] = pair(1 - c, xx).astype(BF)
            send(s0s.at[xx], s0r.at[xx], p0 + k, other)
        for k, d in enumerate((1, 2, 3, 0)):
            xx = (x + d) % 4
            total = pair(c, xx)
            arrived(s0r.at[xx], p0 + k)
            s0[xx] = (total + s0r[xx].astype(F32)).astype(BF)
            if d:
                send(s0.at[xx, 1], r1x.at[d - 1], px + d - 1, to_x(d))
            for e in (1, 2, 3):
                send(s0.at[xx, 0, (y + e) % 4], r1y.at[e - 1, xx], py + 3 * k + e - 1, to_y(e))

        def sum_t1(k, xx):
            total = s0[xx, 0, y].astype(F32)
            for e in (1, 2, 3):
                arrived(r1y.at[e - 1, xx], py + 3 * k + e - 1)
                total = total + r1y[e - 1, xx].astype(F32)
            return total

        def sum_t2(q):
            total = s0[x, 1, q].astype(F32)
            for d in (1, 2, 3):
                total = total + r1x[d - 1, q].astype(F32)
            return total

        for k, d in enumerate((1, 2, 3)):
            xx = (x + d) % 4
            t1[xx] = sum_t1(k, xx).astype(BF)
            send(t1.at[xx], r2x.at[d - 1], qx + d - 1, to_x(d))
        for d in (1, 2, 3):
            arrived(r1x.at[d - 1], px + d - 1)
        for e in (1, 2, 3):
            q = (y + e) % 4
            t2[q] = sum_t2(q).astype(BF)
            send(t2.at[q], r2y.at[e - 1], qy + e - 1, to_y(e))
        w0 = sum_t1(3, x)
        w1 = sum_t2(y)
        for d in (1, 2, 3):
            arrived(r2x.at[d - 1], qx + d - 1)
            w0 = w0 + r2x[d - 1].astype(F32)
        for d in (1, 2, 3):
            arrived(r2y.at[d - 1], qy + d - 1)
            w1 = w1 + r2y[d - 1].astype(F32)
        half = tr // 2
        for h, part_sum in enumerate((w0[:half], w0[half:], w1[:half], w1[half:])):
            wf[h] = part_sum
            wb[h] = part_sum.astype(BF)
        for d in (1, 2, 3):
            send(wb.at[(zh + d) % 4], r3.at[d - 1], p3 + d - 1, to_z(4 * d))
        total = wf[zh]
        for d in (1, 2, 3):
            arrived(r3.at[d - 1], p3 + d - 1)
            total = total + r3[d - 1].astype(F32)
        return total

    def pick(shape, kdim):
        k = lax.broadcasted_iota(jnp.int32, shape, kdim)
        m = lax.broadcasted_iota(jnp.int32, shape, 1 - kdim)
        return jnp.where(k == m // 32 * 128 + y * 32 + m % 32, 1.0, 0.0).astype(BF)

    other_core = gather(va, True)
    load_r.wait()
    load_l.wait()
    pick_t = pick((128, 512), 1)
    for t in range(3):
        rsel[pl.ds(128 * t, 128)] = dot(pick_t, rf[t], NT).astype(BF)
    pick_n = pick((512, 128), 0)
    for t in range(3):
        chosen = dot(lf[t], pick_n, NN).astype(BF)
        for zz in range(4):
            for q in range(4):
                for rh in range(2):
                    a = zz * 128 + q * 32 + rh * 16
                    b = q * 128 + rh * 64 + zz * 16
                    lsel[b : b + 16, 128 * t : 128 * t + 128] = chosen[a : a + 16]

    def left_half(cc):
        lrows = jnp.concatenate([lf[t, pl.ds(zl * 128, 128)] for t in range(3)], axis=0)

        def body(xx, carry):
            src = [va[:, cc, xx, pl.ds(2 * bp, 2)].reshape(128, 512) for bp in range(2)]
            res = dot(lrows, jnp.concatenate(src, axis=0), NT).astype(BF)
            for t in range(3):
                for bp in range(2):
                    mid[t, cc * 8 + xx * 2 + bp] = res[128 * t : 128 * t + 128, 128 * bp : 128 * bp + 128]
            return carry

        lax.fori_loop(0, 4, body, 0)

    left_half(c)
    other_core()
    left_half(1 - c)

    def pair1(cc, xx):
        rows = []
        for bp in range(2):
            b = cc * 8 + xx * 2 + bp
            rows.append(jnp.concatenate([mid[t, pat[t, b]] for t in range(3)], axis=1))
        res = dot(jnp.concatenate(rows, axis=0), rsel[...], NN)
        return res.reshape(2, 4, 32, 512)

    total = reduce(pair1, 32, 512, s0s1, s0r1, s01, r1y1, r1x1, t11, t21, r2x1, r2y1, wf1, wb1, r31)
    b_mine = c * 8 + x * 2 + zh // 2
    size = sizes[b_mine]
    rr = lax.broadcasted_iota(jnp.int32, (16, 512), 0) + (zl * 128 + y * 32 + zh % 2 * 16)
    cc_ = lax.broadcasted_iota(jnp.int32, (16, 512), 1)
    piece = jnp.where(jnp.maximum(rr, cc_) < size, total, 0.0).astype(BF)
    f1[...] = piece
    g1 = copies(3)
    for d in (1, 2, 3):
        send(f1, vb.at[zl, c, x, zh], g1 + d - 1, to_z(4 * d))
    vb[zl, c, x, zh] = piece
    for d in (1, 2, 3):
        arrived(vb.at[zl, c, x, (zh + 4 - d) % 4], g1 + d - 1)

    other_core = gather(vb, False)

    def right_half(cc):
        rrows = jnp.concatenate([rf[t, pl.ds(zl * 128, 128)] for t in range(3)], axis=0)

        def body(xx, carry):
            src = [vb[:, cc, xx, pl.ds(2 * bp, 2)].reshape(128, 512) for bp in range(2)]
            res = dot(jnp.concatenate(src, axis=0), rrows, NT).astype(BF)
            for t in range(3):
                for bp in range(2):
                    mid[t, cc * 8 + xx * 2 + bp] = res[128 * bp : 128 * bp + 128, 128 * t : 128 * t + 128]
            return carry

        lax.fori_loop(0, 4, body, 0)

    right_half(c)
    other_core()
    store1 = pltpu.make_async_copy(vb.at[zl], out1, lsem.at[3])
    store1.start()
    right_half(1 - c)

    def pair2(cc, xx):
        cols = []
        for bp in range(2):
            b = cc * 8 + xx * 2 + bp
            cols.append(jnp.concatenate([mid[t, pat[t, b]] for t in range(3)], axis=0))
        res = dot(lsel[...], jnp.concatenate(cols, axis=1), NN)
        return jnp.stack([res[:, :128].reshape(4, 128, 128), res[:, 128:].reshape(4, 128, 128)])

    total = reduce(pair2, 128, 128, s0s2, s0r2, s02, r1y2, r1x2, t12, t22, r2x2, r2y2, wf2, wb2, r32)
    total = total.reshape(4, 16, 128)
    rr = lax.broadcasted_iota(jnp.int32, (4, 16, 128), 0) * 128 + lax.broadcasted_iota(jnp.int32, (4, 16, 128), 1)
    rr = rr + (y * 32 + zh % 2 * 16)
    cc_ = lax.broadcasted_iota(jnp.int32, (4, 16, 128), 2) + zl * 128
    piece = jnp.where(jnp.maximum(rr, cc_) < size, total, 0.0).astype(BF)
    f2[...] = piece
    g2 = copies(16)
    here = obuf.at[c, x, zh, :, pl.ds(pl.multiple_of(zl * 128, 128), 128)]
    own = pltpu.make_async_copy(f2.at[zl], here, lsem.at[4])
    own.start()
    for dl in range(4):
        for dh in range(4):
            if dl or dh:
                send(f2.at[(zl + dl) % 4], here, g2 + 4 * dl + dh, to_zz(dh, dl))
    own.wait()
    for dl in range(4):
        for dh in range(4):
            if dl or dh:
                zz = (zl + 4 - dl) % 4
                there = obuf.at[c, x, (zh + 4 - dh) % 4, :, pl.ds(pl.multiple_of(zz * 128, 128), 128)]
                arrived(there, g2 + 4 * dl + dh)
    gx, gc = copies(3), copies(4)
    for d in (1, 2, 3):
        send(obuf.at[c, x], obuf.at[c, x], gx + d - 1, to_x(d))
    send(obuf.at[c, x], obuf.at[c, x], gc, other)
    for d in (1, 3, 2):
        xx = (x + 4 - d) % 4
        arrived(obuf.at[c, xx], gx + d - 1)
        send(obuf.at[c, xx], obuf.at[c, xx], gc + d, other)
    for d in range(4):
        arrived(obuf.at[1 - c, (x + 4 - d) % 4], gc + d)
    store2 = pltpu.make_async_copy(obuf, out2, lsem.at[5])
    store2.start()
    for cp in sent:
        cp.wait_send()
    store1.wait()
    store2.wait()


N_COPIES = 39 + 28 + 3 + 39 + 28 + 16 + 7


def on_device(wave_t, left_ops, right_ops, pattern, sector_size):
    def stage(tr, tc):
        return [
            pltpu.VMEM((4, 2, 4, tr, tc), BF),
            pltpu.VMEM((4, 2, 4, tr, tc), BF),
            pltpu.VMEM((4, 2, 4, tr, tc), BF),
            pltpu.VMEM((3, 4, tr, tc), BF),
            pltpu.VMEM((3, 4, tr, tc), BF),
            pltpu.VMEM((4, tr, tc), BF),
            pltpu.VMEM((4, tr, tc), BF),
            pltpu.VMEM((3, tr, tc), BF),
            pltpu.VMEM((3, tr, tc), BF),
            pltpu.VMEM((4, tr // 2, tc), F32),
            pltpu.VMEM((4, tr // 2, tc), BF),
            pltpu.VMEM((3, tr // 2, tc), BF),
        ]

    hbm = pl.BlockSpec(memory_space=pl.ANY)
    smem = pl.BlockSpec(memory_space=pltpu.SMEM)
    out = jax.ShapeDtypeStruct((2, 4, 4, 16, 512), BF)
    first, second = pl.pallas_call(
        kernel,
        out_shape=(out, out),
        in_specs=[hbm, hbm, hbm, smem, smem],
        out_specs=(hbm, hbm),
        scratch_shapes=[
            pltpu.VMEM((2, 4, 4, 16, 512), BF),
            pltpu.VMEM((3, 512, 512), BF),
            pltpu.VMEM((3, 512, 512), BF),
            pltpu.VMEM((384, 512), BF),
            pltpu.VMEM((512, 384), BF),
            pltpu.VMEM((4, 2, 4, 4, 16, 512), BF),
            pltpu.VMEM((4, 2, 4, 4, 16, 512), BF),
            pltpu.VMEM((3, 16, 128, 128), BF),
            *stage(32, 512),
            pltpu.VMEM((16, 512), BF),
            *stage(128, 128),
            pltpu.VMEM((4, 16, 128), BF),
            pltpu.VMEM((2, 4, 4, 16, 512), BF),
            pltpu.SemaphoreType.DMA((6,)),
            pltpu.SemaphoreType.DMA((N_COPIES,)),
            pltpu.SemaphoreType.DMA((N_COPIES,)),
        ],
        compiler_params=pltpu.CompilerParams(
            collective_id=0, has_side_effects=True, vmem_limit_bytes=48 * 2**20
        ),
        name="hamiltonian",
    )(wave_t.reshape(2, 4, 4, 16, 512), left_ops, right_ops, pattern, sector_size)
    return first.reshape(16, 32, 512), second.reshape(16, 32, 512)


def solution(mesh):
    return jax.shard_map(
        on_device,
        mesh=mesh,
        in_specs=(
            P(None, "sec", None),
            P("ops", None, None),
            P("ops", None, None),
            P("ops", None),
            P(),
        ),
        out_specs=(P(None, "sec", None), P(None, "sec", None)),
        check_vma=False,
    )
```

time: 625 us -> 121 us (0.19); the launches traced: 615 us -> 121 us
  blocking collectives: 359 us -> 0 us
  waiting for transfers between devices: 218 us -> 0 us
  Pallas kernels: 0 us -> 114 us
  matrix products: 16.7 us -> 0 us
  between operations: 14.1 us -> 0.65 us
    psum x2 -> x0, blocking collectives: 359 us -> none  [combine_terms(): summed = lax.psum(partial_rows, 'ops')]
    all_gather x2 -> x0, waiting for transfers between devices: 218 us -> none  [the longest x1 113 us: on_device(): full_wave = lax.all_gather(columns_t, 'sec', axis=1, tiled=True)]
    pallas_call x0 -> x1, Pallas kernels: none -> 114 us  [on_device(): pl.pallas_call(kernel, out_shape=(out, out), in_specs=[hbm, hbm, hbm, sme...]
    dot_general x4 -> x0, matrix products: 16.7 us -> none  [the longest x1 6.01 us: on_device(): jnp.einsum('tij,bcj->tbic', rows_left, full_wave, preferred_element_type=...]
    unnamed x4 -> x12, local copies, waits for them, and re-layouts: 0.01 us -> 6.77 us
  transfers between devices with their start and end apart: 2 -> 0, of which waited for: 2 -> 0; matrix products, arithmetic and copies ran while one was open for 0% -> 0% of each run, Pallas kernels for 0% -> 0%
where the time goes in v1:
time: 121 us
  Pallas kernels  114 us (94%)
  local copies, waits for them, and re-layouts  6.77 us (6%)
    pallas_call x1, Pallas kernels, on_device(): pl.pallas_call(kernel, out_shape=(out, out), in_specs=[hbm, hbm, hbm, sme...  114 us
    unnamed x12, local copies, waits for them, and re-layouts  6.77 us

profile of v1, /device:TPU:1, one launch (start us, length us, event | category | flops | bytes accessed | tf_op | source)
XLA Modules:
  0.0 121.0 jit_solution(336078739202572668)
XLA Ops:
  0.6 0.0 copy-start
  0.6 1.4 %copy-done = bf16[3,512,512]{2,1,0:T(8,128)(2,1)S(1)} copy-done((bf16[3,512,512]{2,1,0:T(8,128)(2,1)S(1)}, bf16[3,512,512]{2,1,0:T(8,128)(2,1)}, u32[]{:S(2)}) %copy-start) | copy-done | bytes 1572888
  2.0 0.0 copy-start.1
  2.0 1.4 %copy-done.1 = bf16[3,512,512]{2,1,0:T(8,128)(2,1)S(1)} copy-done((bf16[3,512,512]{2,1,0:T(8,128)(2,1)S(1)}, bf16[3,512,512]{2,1,0:T(8,128)(2,1)}, u32[]{:S(2)}) %copy-start.1) | copy-done | bytes 1572888
  3.4 0.0 copy-start.2
  3.5 1.0 copy-done.2
  4.5 0.0 copy-start.3
  4.5 0.7 copy-done.3
  5.2 0.0 copy-start.4
  5.2 0.7 copy-done.4
  5.8 113.6 %hamiltonian.1 = (bf16[2,4,4,16,512]{4,3,2,1,0:T(8,128)(2,1)S(1)}, bf16[2,4,4,16,512]{4,3,2,1,0:T(8,128)(2,1)S(1)}) custom-call(bf16[2,4,4,16,512]{4,3,2,1,0:T(8,128)(2,1)S(1)} %bitcast.3, bf16[3,512,512]{2,1,0:T(8,128)(2,1)S(1)} %copy-done, bf16[3,512,512]{2,1,0:T(8,128)(2,1)S(1)} %copy-done.1, s32[3,16]{1,0:T(4,128)S(1)} %copy-done.3, s32[16]{0:T(128)S(1)} %copy-done.4), custom_call_target="tpu_custom_call" | custom-call | tf_op jit(solution)/shard_map/hamiltonian/pallas_call | solution.py:375
  119.4 0.8 copy.9
  120.2 0.8 copy.10
Async XLA Ops:
  0.6 1.4 %copy-start = (bf16[3,512,512]{2,1,0:T(8,128)(2,1)S(1)}, bf16[3,512,512]{2,1,0:T(8,128)(2,1)}, u32[]{:S(2)}) copy-start(bf16[3,512,512]{2,1,0:T(8,128)(2,1)} %lops.1) | copy-start | bytes 4718596
  2.0 1.4 %copy-start.1 = (bf16[3,512,512]{2,1,0:T(8,128)(2,1)S(1)}, bf16[3,512,512]{2,1,0:T(8,128)(2,1)}, u32[]{:S(2)}) copy-start(bf16[3,512,512]{2,1,0:T(8,128)(2,1)} %rops.1) | copy-start | bytes 4718596
  3.4 1.0 copy-start.2
  4.5 0.7 copy-start.3
  5.2 0.7 copy-start.4

commit v2 on v1

--- a/solution.py
+++ b/solution.py
@@ -21,7 +21,7 @@
     wbuf, lf, rf, rsel, lsel, va, vb, mid,
     s0s1, s0r1, s01, r1y1, r1x1, t11, t21, r2x1, r2y1, wf1, wb1, r31, f1,
     s0s2, s0r2, s02, r1y2, r1x2, t12, t22, r2x2, r2y2, wf2, wb2, r32, f2,
-    obuf, lsem, ssem, rsem,
+    obuf, lsem, ssem, rsem, relay,
 ):
     ops, sec = lax.axis_index("ops"), lax.axis_index("sec")
     x, zh, c = ops // 8, (ops // 2) % 4, ops % 2
@@ -68,7 +68,7 @@
     load_w.start()
     load_r.start()
     load_l.start()
-    partners = [other] + [to_y(d) for d in (1, 2, 3)] + [to_x(d) for d in (1, 2, 3)] + [to_z(d) for d in range(1, 16)]
+    partners = [other] + [to_y(d) for d in (1, 2, 3)] + [to_x(d) for d in (1, 2, 3)] + [to_z(d) for d in (1, 2, -2, -1)]
     barrier = pltpu.get_barrier_semaphore()
     for device in partners:
         pl.semaphore_signal(barrier, inc=1, device_id=device, device_id_type=MESH)
@@ -88,6 +88,8 @@
 
     lax.fori_loop(0, 8, mask_wave, 0)
     pl.semaphore_wait(barrier, len(partners))
+    for d in (2, -2):
+        pl.semaphore_signal(relay.at[0], inc=1, device_id=to_z(d), device_id_type=MESH)
 
     z_of = [zl, (zl + 3) % 4, (zl + 1) % 4, (zl + 2) % 4]
 
@@ -177,6 +179,7 @@
             for e in (1, 2, 3):
                 send(s0.at[xx, 0, (y + e) % 4], r1y.at[e - 1, xx], py + 3 * k + e - 1, to_y(e))
 
+
         def sum_t1(k, xx):
             total = s0[xx, 0, y].astype(F32)
             for e in (1, 2, 3):
@@ -208,6 +211,8 @@
         for d in (1, 2, 3):
             arrived(r2y.at[d - 1], qy + d - 1)
             w1 = w1 + r2y[d - 1].astype(F32)
+        if tr == 32:
+            pl.semaphore_wait(relay.at[1], 2)
         half = tr // 2
         for h, part_sum in enumerate((w0[:half], w0[half:], w1[:half], w1[half:])):
             wf[h] = part_sum
@@ -257,6 +262,9 @@
     left_half(c)
     other_core()
     left_half(1 - c)
+    pl.semaphore_wait(relay.at[0], 2)
+    for d in (4, -4):
+        pl.semaphore_signal(relay.at[1], inc=1, device_id=to_z(d), device_id_type=MESH)
 
     def pair1(cc, xx):
         rows = []
@@ -343,10 +351,10 @@
         arrived(obuf.at[1 - c, (x + 4 - d) % 4], gc + d)
     store2 = pltpu.make_async_copy(obuf, out2, lsem.at[5])
     store2.start()
+    store1.wait()
+    store2.wait()
     for cp in sent:
         cp.wait_send()
-    store1.wait()
-    store2.wait()
 
 
 N_COPIES = 39 + 28 + 3 + 39 + 28 + 16 + 7
@@ -370,12 +378,13 @@
         ]
 
     hbm = pl.BlockSpec(memory_space=pl.ANY)
+    fixed = pl.BlockSpec(memory_space=pltpu.HBM)
     smem = pl.BlockSpec(memory_space=pltpu.SMEM)
     out = jax.ShapeDtypeStruct((2, 4, 4, 16, 512), BF)
     first, second = pl.pallas_call(
         kernel,
         out_shape=(out, out),
-        in_specs=[hbm, hbm, hbm, smem, smem],
+        in_specs=[fixed, fixed, fixed, smem, smem],
         out_specs=(hbm, hbm),
         scratch_shapes=[
             pltpu.VMEM((2, 4, 4, 16, 512), BF),
@@ -394,6 +403,7 @@
             pltpu.SemaphoreType.DMA((6,)),
             pltpu.SemaphoreType.DMA((N_COPIES,)),
             pltpu.SemaphoreType.DMA((N_COPIES,)),
+            pltpu.SemaphoreType.REGULAR((2,)),
         ],
         compiler_params=pltpu.CompilerParams(
             collective_id=0, has_side_effects=True, vmem_limit_bytes=48 * 2**20

time: 121 us -> 117 us (0.967)
  Pallas kernels: 114 us -> 109 us
    pallas_call x1, Pallas kernels: 114 us -> 109 us  [on_device(): pl.pallas_call(kernel, out_shape=(out, out), in_specs=[fixed, fixed, fixe...]
where the time goes in v2:
time: 117 us; the launch traced here: 116 us
  Pallas kernels  109 us (93%)
  local copies, waits for them, and re-layouts  6.77 us (6%)
    pallas_call x1, Pallas kernels, on_device(): pl.pallas_call(kernel, out_shape=(out, out), in_specs=[fixed, fixed, fixe...  109 us
    unnamed x12, local copies, waits for them, and re-layouts  6.77 us

profile of v2, /device:TPU:1, one launch (start us, length us, event | category | flops | bytes accessed | tf_op | source)
XLA Modules:
  0.0 116.4 jit_solution(10822662971587941940)
XLA Ops:
  0.6 0.0 copy-start
  0.6 1.4 %copy-done = bf16[3,512,512]{2,1,0:T(8,128)(2,1)S(1)} copy-done((bf16[3,512,512]{2,1,0:T(8,128)(2,1)S(1)}, bf16[3,512,512]{2,1,0:T(8,128)(2,1)}, u32[]{:S(2)}) %copy-start) | copy-done | bytes 1572888
  2.0 0.0 copy-start.1
  2.0 1.4 %copy-done.1 = bf16[3,512,512]{2,1,0:T(8,128)(2,1)S(1)} copy-done((bf16[3,512,512]{2,1,0:T(8,128)(2,1)S(1)}, bf16[3,512,512]{2,1,0:T(8,128)(2,1)}, u32[]{:S(2)}) %copy-start.1) | copy-done | bytes 1572888
  3.4 0.0 copy-start.2
  3.5 1.0 copy-done.2
  4.5 0.0 copy-start.3
  4.5 0.7 copy-done.3
  5.2 0.0 copy-start.4
  5.2 0.7 copy-done.4
  5.8 109.0 %hamiltonian.1 = (bf16[2,4,4,16,512]{4,3,2,1,0:T(8,128)(2,1)S(1)}, bf16[2,4,4,16,512]{4,3,2,1,0:T(8,128)(2,1)S(1)}) custom-call(bf16[2,4,4,16,512]{4,3,2,1,0:T(8,128)(2,1)S(1)} %bitcast.3, bf16[3,512,512]{2,1,0:T(8,128)(2,1)S(1)} %copy-done, bf16[3,512,512]{2,1,0:T(8,128)(2,1)S(1)} %copy-done.1, s32[3,16]{1,0:T(4,128)S(1)} %copy-done.3, s32[16]{0:T(128)S(1)} %copy-done.4), custom_call_target="tpu_custom_call" | custom-call | tf_op jit(solution)/shard_map/hamiltonian/pallas_call | solution.py:384
  114.8 0.8 copy.9
  115.6 0.8 copy.10
Async XLA Ops:
  0.6 1.4 %copy-start = (bf16[3,512,512]{2,1,0:T(8,128)(2,1)S(1)}, bf16[3,512,512]{2,1,0:T(8,128)(2,1)}, u32[]{:S(2)}) copy-start(bf16[3,512,512]{2,1,0:T(8,128)(2,1)} %lops.1) | copy-start | bytes 4718596
  2.0 1.4 %copy-start.1 = (bf16[3,512,512]{2,1,0:T(8,128)(2,1)S(1)}, bf16[3,512,512]{2,1,0:T(8,128)(2,1)}, u32[]{:S(2)}) copy-start(bf16[3,512,512]{2,1,0:T(8,128)(2,1)} %rops.1) | copy-start | bytes 4718596
  3.4 1.0 copy-start.2
  4.5 0.7 copy-start.3
  5.2 0.7 copy-start.4

commit v3 on v0

v3 whole, which is shorter than its diff:
```python
import jax
import jax.numpy as jnp
from jax import lax
from jax.experimental import pallas as pl
from jax.experimental.pallas import tpu as pltpu
from jax.sharding import PartitionSpec as P

MESH = pl.DeviceIdType.MESH
BF = jnp.bfloat16
F32 = jnp.float32
NT = (((1,), (1,)), ((), ()))
NN = (((1,), (0,)), ((), ()))
N_STAGE = 13
N_COPIES = 500


def dot(a, b, dims):
    return lax.dot_general(a, b, dims, preferred_element_type=F32)


def kernel(wave, lops, rops, pat, sizes, out1, out2, *scratch):
    wbuf, lf, rf, rsel, lsel, va, vb, mid, f1, f2, obuf, lsem, ssem, rsem, relay = scratch[: -2 * N_STAGE]
    stage1, stage2 = scratch[-2 * N_STAGE : -N_STAGE], scratch[-N_STAGE:]
    ops, sec = lax.axis_index("ops"), lax.axis_index("sec")
    x, zh, c = ops // 8, (ops // 2) % 4, ops % 2
    zl, y = sec // 4, sec % 4
    z = zh * 4 + zl

    def to_x(d):
        return {"ops": ((x + d) % 4 * 4 + zh) * 2 + c, "sec": sec}

    def to_y(d):
        return {"ops": ops, "sec": zl * 4 + (y + d) % 4}

    def to_z(d):
        w = (z + d + 16) % 16
        return {"ops": (x * 4 + w // 4) * 2 + c, "sec": w % 4 * 4 + y}

    other = {"ops": ops + 1 - 2 * c, "sec": sec}

    sent = []
    relayed = [2]
    count = [0]

    def copies(n):
        first = count[0]
        count[0] += n
        return first

    def remote(src, dst, index, device, out_index=None):
        return pltpu.make_async_remote_copy(
            src_ref=src, dst_ref=dst, send_sem=ssem.at[index if out_index is None else out_index], recv_sem=rsem.at[index],
            device_id=device, device_id_type=MESH,
        )

    def send(src, dst, index, device, out_index=None):
        cp = remote(src, dst, index, device, out_index)
        cp.start()
        sent.append(cp)

    def arrived(ref, index):
        pltpu.make_async_copy(ref, ref, rsem.at[index]).wait()

    load_w = pltpu.make_async_copy(wave, wbuf, lsem.at[0])
    load_r = pltpu.make_async_copy(rops, rf, lsem.at[1])
    load_l = pltpu.make_async_copy(lops, lf, lsem.at[2])
    load_w.start()
    load_r.start()
    load_l.start()
    partners = [other] + [to_y(d) for d in (1, 2, 3)] + [to_x(d) for d in (1, 2, 3)] + [to_z(d) for d in (1, 2, -2, -1)]
    barrier = pltpu.get_barrier_semaphore()
    for device in partners:
        pl.semaphore_signal(barrier, inc=1, device_id=device, device_id_type=MESH)

    load_w.wait()
    row = lax.broadcasted_iota(jnp.int32, (16, 512), 0) + (zl * 128 + y * 32)
    col = lax.broadcasted_iota(jnp.int32, (16, 512), 1)

    def mask_wave(k, carry):
        cc, xx = k // 4, k % 4
        for rh in range(2):
            edge = jnp.maximum(row + 16 * rh, col)
            for bp in range(2):
                block = wbuf[cc, xx, bp, rh].astype(F32)
                va[zl, cc, xx, rh, bp] = jnp.where(edge < sizes[2 * k + bp], block, 0.0).astype(BF)
        return carry

    lax.fori_loop(0, 8, mask_wave, 0)
    pl.semaphore_wait(barrier, len(partners))
    for d in (2, -2):
        pl.semaphore_signal(relay.at[0], inc=1, device_id=to_z(d), device_id_type=MESH)

    z_of = [zl, (zl + 3) % 4, (zl + 1) % 4, (zl + 2) % 4]
    x_of = [x, (x + 3) % 4, (x + 1) % 4, (x + 2) % 4]
    step = [0, 1, 3, 2]

    def gather(v, chunk, whole_slab):
        halves = (0, 1) if chunk is None else (chunk,)
        rows = pl.ds(halves[0], len(halves))
        a1, b1, a2, b2, cx = copies(4), copies(3), copies(12), copies(16), copies(4)

        def z_send(xx, bp, i0):
            block = v.at[zl, c, xx, rows, bp]
            send(block, block, i0, to_z(1))
            send(block, block, i0 + 1, to_z(-1))
            for rh in halves:
                block = v.at[zl, c, xx, rh, bp]
                send(block, block, i0 + 2 + rh, to_z(2 - 4 * rh))

        def z_arrived(xx, bp, k, i0):
            if k < 3:
                arrived(v.at[z_of[k], c, xx, rows, bp], i0 + k - 1)
            else:
                for rh in halves:
                    arrived(v.at[z_of[k], c, xx, rh, bp], i0 + 2 + rh)

        def x_send(zz, bp, i0):
            block = v.at[zz, c, x, rows, bp]
            for d in (1, 2, 3):
                send(block, block, i0 + d - 1, to_x(d))

        z_send(x, 0, a1)
        if whole_slab:
            for k in range(4):
                z_send(x_of[k], 1, b2 + 4 * k)
        else:
            x_send(zl, 1, b1)
            x_send(zl, 0, a2)
            z_send(x, 1, b2)
        yield
        for k in (1, 2, 3):
            if not whole_slab:
                arrived(v.at[zl, c, x_of[k], rows, 1], b1 + step[k] - 1)
                z_send(x_of[k], 1, b2 + 4 * k)
            z_arrived(x, 0, k, a1)
            x_send(z_of[k], 0, a2 + 3 * k)
        yield
        for k in range(4):
            if k == 0 and whole_slab:
                continue
            for m in (1, 2, 3):
                arrived(v.at[z_of[k], c, x_of[m], rows, 0], a2 + 3 * k + step[m] - 1)
            if k > 0:
                for m in range(4):
                    z_arrived(x_of[m], 1, k, b2 + 4 * m)
            block = v.at[z_of[k], c, :, rows]
            send(block, block, cx + k, other)
        yield
        for k in range(4):
            if k == 0 and whole_slab:
                continue
            arrived(v.at[z_of[k], 1 - c, :, rows], cx + k)
        yield

    def run(flows, steps):
        for _ in range(steps):
            for flow in flows:
                next(flow)

    def drain():
        while sent:
            sent.pop().wait_send()

    def reduce(pair, half, cut, finish, s0s, s0r, s0, r1y, r1x, t1, t2, t2b, r2x, r2y, wf, wb, r3):
        p0, py, px, qx, qy, p3 = copies(4), copies(12), copies(6), copies(6), copies(6), copies(6)
        for k, d in enumerate((1, 2, 3, 0)):
            s0s[k] = pair(1 - c, (x + d) % 4).astype(BF)
            send(s0s.at[k], s0r.at[k], p0 + k, other)

        def first_sends(k, ch):
            if k < 3:
                send(s0.at[k, ch, 1], r1x.at[ch, k], px + 3 * ch + k, to_x(k + 1))
            if k % 2:
                for e in (1, 2, 3):
                    q = (y + e) % 4
                    send(s0.at[pl.ds(k - 1, 2), ch, 0, q], r1y.at[ch, e - 1, pl.ds(k - 1, 2)],
                         py + 6 * ch + 3 * (k // 2) + e - 1, to_y(e))

        for k, d in enumerate((1, 2, 3, 0)):
            total = pair(c, (x + d) % 4)
            arrived(s0r.at[k], p0 + k)
            total = total + s0r[k].astype(F32)
            for ch in range(2):
                for bp in range(2):
                    s0[k, ch, bp] = total[bp, :, ch * half : (ch + 1) * half].astype(BF)
            first_sends(k, 0)
        for k in range(4):
            first_sends(k, 1)

        def flow(ch):
            def sum_t1(k):
                total = s0[k, ch, 0, y].astype(F32)
                for e in (1, 2, 3):
                    total = total + r1y[ch, e - 1, k].astype(F32)
                return total

            for k in range(4):
                if k % 2 == 0:
                    for e in (1, 2, 3):
                        arrived(r1y.at[ch, e - 1, pl.ds(k, 2)], py + 6 * ch + 3 * (k // 2) + e - 1)
                if k < 3:
                    t1[ch, k] = sum_t1(k).astype(BF)
                    send(t1.at[ch, k], r2x.at[ch, k], qx + 3 * ch + k, to_x(k + 1))
            for k in range(3):
                arrived(r1x.at[ch, k], px + 3 * ch + k)
            mine = s0[3, ch, 1].astype(F32)
            for k in range(3):
                mine = mine + r1x[ch, k].astype(F32)
            t2[ch] = mine
            for e in (1, 2, 3):
                q = (y + e) % 4
                t2b[ch, e - 1] = t2[ch, q].astype(BF)
                send(t2b.at[ch, e - 1], r2y.at[ch, e - 1], qy + 3 * ch + e - 1, to_y(e))
            yield
            w0 = sum_t1(3)
            w1 = t2[ch, y]
            for k in range(3):
                arrived(r2x.at[ch, k], qx + 3 * ch + k)
                w0 = w0 + r2x[ch, k].astype(F32)
            for k in range(3):
                arrived(r2y.at[ch, k], qy + 3 * ch + k)
                w1 = w1 + r2y[ch, k].astype(F32)
            if relayed:
                pl.semaphore_wait(relay.at[1], relayed.pop())
            for bp, w in enumerate((w0, w1)):
                for part in range(2):
                    piece = cut(w, part)
                    wf[ch, 2 * bp + part] = piece
                    wb[ch, 2 * bp + part] = piece.astype(BF)
            for d in (1, 3, 2):
                send(wb.at[ch, (zh + d) % 4], r3.at[ch, d - 1], p3 + 3 * ch + d - 1, to_z(4 * d))
            yield
            total = wf[ch, zh]
            for d in (1, 3, 2):
                arrived(r3.at[ch, d - 1], p3 + 3 * ch + d - 1)
                total = total + r3[ch, d - 1].astype(F32)
            yield from finish(ch, total)

        return [flow(0), flow(1)]

    def pick(shape, kdim):
        k = lax.broadcasted_iota(jnp.int32, shape, kdim)
        m = lax.broadcasted_iota(jnp.int32, shape, 1 - kdim)
        return jnp.where(k == m // 32 * 128 + y * 32 + m % 32, 1.0, 0.0).astype(BF)

    start = gather(va, None, True)
    next(start)
    load_r.wait()
    load_l.wait()
    pick_t = pick((128, 512), 1)
    for t in range(3):
        rsel[pl.ds(128 * t, 128)] = dot(pick_t, rf[t], NT).astype(BF)
    next(start)
    next(start)

    def left_half(cc):
        lrows = jnp.concatenate([lf[t, pl.ds(zl * 128, 128)] for t in range(3)], axis=0)

        def body(xx, carry):
            src = [va[:, cc, xx, :, bp].reshape(128, 512) for bp in range(2)]
            res = dot(lrows, jnp.concatenate(src, axis=0), NT).astype(BF)
            for t in range(3):
                for bp in range(2):
                    mid[t, cc * 8 + xx * 2 + bp] = res[128 * t : 128 * t + 128, 128 * bp : 128 * bp + 128]
            return carry

        lax.fori_loop(0, 4, body, 0)

    left_half(c)
    next(start)
    left_half(1 - c)
    pl.semaphore_wait(relay.at[0], 2)
    for d in (4, -4):
        pl.semaphore_signal(relay.at[1], inc=1, device_id=to_z(d), device_id_type=MESH)

    def pair1(cc, xx):
        rows = []
        for bp in range(2):
            b = cc * 8 + xx * 2 + bp
            rows.append(jnp.concatenate([mid[t, pat[t, b]] for t in range(3)], axis=1))
        res = dot(jnp.concatenate(rows, axis=0), rsel[...], NN)
        return res.reshape(2, 4, 32, 512)

    b_mine = c * 8 + x * 2 + zh // 2

    def columns(part):
        return pl.ds(pl.multiple_of(part * 256, 256), 256)

    def finish1(ch, total):
        rr = lax.broadcasted_iota(jnp.int32, (16, 256), 0) + (zl * 128 + y * 32 + 16 * ch)
        cc_ = lax.broadcasted_iota(jnp.int32, (16, 256), 1) + zh % 2 * 256
        f1[ch] = jnp.where(jnp.maximum(rr, cc_) < sizes[b_mine], total, 0.0).astype(BF)
        here = vb.at[zl, c, x, ch, zh // 2, :, columns(zh % 2)]
        own = pltpu.make_async_copy(f1.at[ch], here, lsem.at[3 + ch])
        own.start()
        g1 = copies(3)
        for d in (1, 3, 2):
            send(f1.at[ch], here, g1 + d - 1, to_z(4 * d))
        yield
        own.wait()
        for d in (1, 3, 2):
            h = (zh + 4 - d) % 4
            arrived(vb.at[zl, c, x, ch, h // 2, :, columns(h % 2)], g1 + d - 1)
        yield from gather(vb, ch, False)

    flows = reduce(pair1, 16, lambda w, part: w[:, 256 * part : 256 * part + 256], finish1, *stage1)
    pick_n = pick((512, 128), 0)
    run(flows, 1)
    for t in range(3):
        chosen = dot(lf[t], pick_n, NN).astype(BF)
        for zz in range(4):
            for q in range(4):
                for rh in range(2):
                    a = zz * 128 + q * 32 + rh * 16
                    b = q * 128 + rh * 64 + zz * 16
                    lsel[b : b + 16, 128 * t : 128 * t + 128] = chosen[a : a + 16]
    run(flows, 5)

    def right_half(cc):
        rrows = jnp.concatenate([rf[t, pl.ds(zl * 128, 128)] for t in range(3)], axis=0)

        def body(xx, carry):
            src = [vb[:, cc, xx, :, bp].reshape(128, 512) for bp in range(2)]
            res = dot(jnp.concatenate(src, axis=0), rrows, NT).astype(BF)
            for t in range(3):
                for bp in range(2):
                    mid[t, cc * 8 + xx * 2 + bp] = res[128 * bp : 128 * bp + 128, 128 * t : 128 * t + 128]
            return carry

        lax.fori_loop(0, 4, body, 0)

    right_half(c)
    run(flows, 1)
    stores = []

    def store(src, dst, index):
        for rh in range(2):
            for bp in range(2):
                cp = pltpu.make_async_copy(src.at[:, :, rh, bp], dst.at[:, :, bp, rh], lsem.at[index + 2 * rh + bp])
                cp.start()
                stores.append(cp)

    store(vb.at[zl], out1, 5)
    right_half(1 - c)

    def pair2(cc, xx):
        cols = []
        for bp in range(2):
            b = cc * 8 + xx * 2 + bp
            cols.append(jnp.concatenate([mid[t, pat[t, b]] for t in range(3)], axis=0))
        res = dot(lsel[...], jnp.concatenate(cols, axis=1), NN)
        return jnp.stack([res[:, :128].reshape(4, 128, 128), res[:, 128:].reshape(4, 128, 128)])

    def finish2(ch, total):
        total = total.reshape(2, 16, 128)
        shape = (2, 16, 128)
        rr = lax.broadcasted_iota(jnp.int32, shape, 0) * 128 + lax.broadcasted_iota(jnp.int32, shape, 1)
        rr = rr + (zh % 2 * 256 + y * 32 + 16 * ch)
        cc_ = lax.broadcasted_iota(jnp.int32, shape, 2) + zl * 128
        f2[ch] = jnp.where(jnp.maximum(rr, cc_) < sizes[b_mine], total, 0.0).astype(BF)
        g2, out = copies(8), copies(8)
        here = obuf.at[c, x, ch, zh // 2, :, pl.ds(pl.multiple_of(zl * 128, 128), 128)]
        for i in range(2):
            to = zh % 2 * 2 + i
            for dh in (0, 1, 3, 2):
                device = {"ops": (x * 4 + (zh + dh) % 4) * 2 + c, "sec": to * 4 + y}
                if dh:
                    send(f2.at[ch, i], here, g2 + 4 * (dh // 2) + zl, device, out + 4 * i + dh)
                else:

                    @pl.when(to != zl)
                    def _():
                        remote(f2.at[ch, i], here, g2 + zl, device, out + 4 * i).start()

                    @pl.when(to == zl)
                    def _():
                        pltpu.make_async_copy(f2.at[ch, i], here, lsem.at[9 + ch]).start()

        yield
        for i in range(2):
            to = zh % 2 * 2 + i

            @pl.when(to != zl)
            def _():
                remote(f2.at[ch, i], here, g2 + zl, other, out + 4 * i).wait_send()

            @pl.when(to == zl)
            def _():
                pltpu.make_async_copy(f2.at[ch, i], here, lsem.at[9 + ch]).wait()

        odd = (zh + zl // 2) % 2
        for j in range(2):
            h = (zh + 4 - 2 * j - odd) % 4
            for zz in range(4):
                there = obuf.at[c, x, ch, h // 2, :, pl.ds(128 * zz, 128)]
                if j:
                    arrived(there, g2 + 4 + zz)
                else:

                    @pl.when((zz != zl) | (odd != 0))
                    def _():
                        arrived(there, g2 + zz)

        gx, gc = copies(3), copies(4)
        block = obuf.at[c, x, ch]
        for d in (1, 2, 3):
            send(block, block, gx + d - 1, to_x(d))
        send(block, block, gc, other)
        yield
        for d in (1, 3, 2):
            block = obuf.at[c, (x + 4 - d) % 4, ch]
            arrived(block, gx + d - 1)
            send(block, block, gc + d, other)
        yield
        for d in range(4):
            arrived(obuf.at[1 - c, (x + 4 - d) % 4, ch], gc + d)
        yield

    flows = reduce(pair2, 64, lambda w, part: w[32 * part : 32 * part + 32], finish2, *stage2)
    run(flows, 2)
    drain()
    run(flows, 4)
    store(obuf, out2, 11)
    drain()
    for cp in stores:
        cp.wait()
    assert count[0] <= N_COPIES, count


def on_device(wave_t, left_ops, right_ops, pattern, sector_size):
    def stage(r, w, piece):
        return [
            pltpu.VMEM((4, 2, 4, 2 * r, w), BF),
            pltpu.VMEM((4, 2, 4, 2 * r, w), BF),
            pltpu.VMEM((4, 2, 2, 4, r, w), BF),
            pltpu.VMEM((2, 3, 4, r, w), BF),
            pltpu.VMEM((2, 3, 4, r, w), BF),
            pltpu.VMEM((2, 3, r, w), BF),
            pltpu.VMEM((2, 4, r, w), F32),
            pltpu.VMEM((2, 3, r, w), BF),
            pltpu.VMEM((2, 3, r, w), BF),
            pltpu.VMEM((2, 3, r, w), BF),
            pltpu.VMEM((2, 4, *piece), F32),
            pltpu.VMEM((2, 4, *piece), BF),
            pltpu.VMEM((2, 3, *piece), BF),
        ]

    hbm = pl.BlockSpec(memory_space=pl.ANY)
    smem = pl.BlockSpec(memory_space=pltpu.SMEM)
    out = jax.ShapeDtypeStruct((2, 4, 2, 2, 16, 512), BF)
    first, second = pl.pallas_call(
        kernel,
        out_shape=(out, out),
        in_specs=[hbm, hbm, hbm, smem, smem],
        out_specs=(hbm, hbm),
        scratch_shapes=[
            pltpu.VMEM((2, 4, 2, 2, 16, 512), BF),
            pltpu.VMEM((3, 512, 512), BF),
            pltpu.VMEM((3, 512, 512), BF),
            pltpu.VMEM((384, 512), BF),
            pltpu.VMEM((512, 384), BF),
            pltpu.VMEM((4, 2, 4, 2, 2, 16, 512), BF),
            pltpu.VMEM((4, 2, 4, 2, 2, 16, 512), BF),
            pltpu.VMEM((3, 16, 128, 128), BF),
            pltpu.VMEM((2, 16, 256), BF),
            pltpu.VMEM((2, 2, 16, 128), BF),
            pltpu.VMEM((2, 4, 2, 2, 16, 512), BF),
            pltpu.SemaphoreType.DMA((16,)),
            pltpu.SemaphoreType.DMA((N_COPIES,)),
            pltpu.SemaphoreType.DMA((N_COPIES,)),
            pltpu.SemaphoreType.REGULAR((2,)),
            *stage(16, 512, (16, 256)),
            *stage(64, 128, (32, 128)),
        ],
        compiler_params=pltpu.CompilerParams(
            collective_id=0, has_side_effects=True, vmem_limit_bytes=58 * 2**20
        ),
        name="hamiltonian",
    )(wave_t.reshape(2, 4, 2, 2, 16, 512), left_ops, right_ops, pattern, sector_size)
    return first.reshape(16, 32, 512), second.reshape(16, 32, 512)


def solution(mesh):
    return jax.shard_map(
        on_device,
        mesh=mesh,
        in_specs=(
            P(None, "sec", None),
            P("ops", None, None),
            P("ops", None, None),
            P("ops", None),
            P(),
        ),
        out_specs=(P(None, "sec", None), P(None, "sec", None)),
        check_vma=False,
    )
```

time: 625 us -> 115 us (0.18); the launches traced: 615 us -> 115 us
  blocking collectives: 359 us -> 0 us
  waiting for transfers between devices: 218 us -> 0 us
  Pallas kernels: 0 us -> 111 us
  matrix products: 16.7 us -> 0 us
  between operations: 14.1 us -> 0.64 us
    psum x2 -> x0, blocking collectives: 359 us -> none  [combine_terms(): summed = lax.psum(partial_rows, 'ops')]
    all_gather x2 -> x0, waiting for transfers between devices: 218 us -> none  [the longest x1 113 us: on_device(): full_wave = lax.all_gather(columns_t, 'sec', axis=1, tiled=True)]
    pallas_call x0 -> x1, Pallas kernels: none -> 111 us  [on_device(): pl.pallas_call(kernel, out_shape=(out, out), in_specs=[hbm, hbm, hbm, sme...]
    dot_general x4 -> x0, matrix products: 16.7 us -> none  [the longest x1 6.01 us: on_device(): jnp.einsum('tij,bcj->tbic', rows_left, full_wave, preferred_element_type=...]
  transfers between devices with their start and end apart: 2 -> 0, of which waited for: 2 -> 0; matrix products, arithmetic and copies ran while one was open for 0% -> 0% of each run, Pallas kernels for 0% -> 0%
where the time goes in v3:
time: 115 us
  Pallas kernels  111 us (97%)
  local copies, waits for them, and re-layouts  3.76 us (3%)
    pallas_call x1, Pallas kernels, on_device(): pl.pallas_call(kernel, out_shape=(out, out), in_specs=[hbm, hbm, hbm, sme...  111 us
    unnamed x2, local copies, waits for them, and re-layouts  3.76 us

profile of v3, /device:TPU:1, one launch (start us, length us, event | category | flops | bytes accessed | tf_op | source)
XLA Modules:
  0.0 115.0 jit_solution(3161944629732413883)
XLA Ops:
  0.6 110.6 %hamiltonian.1 = (bf16[2,4,2,2,16,512]{5,4,3,2,1,0:T(8,128)(2,1)}, bf16[2,4,2,2,16,512]{5,4,3,2,1,0:T(8,128)(2,1)}) custom-call(bf16[2,4,2,2,16,512]{5,4,3,2,1,0:T(8,128)(2,1)} %bitcast.3, bf16[3,512,512]{2,1,0:T(8,128)(2,1)} %lops.1, bf16[3,512,512]{2,1,0:T(8,128)(2,1)} %rops.1, s32[3,16]{1,0:T(4,128)} %pat.1, s32[16]{0:T(128)} %sizes.1), custom_call_target="tpu_custom_call" | custom-call | tf_op jit(solution)/shard_map/hamiltonian/pallas_call | solution.py:451
  111.3 1.9 %copy.9 = bf16[16,32,512]{2,1,0:T(8,128)(2,1)} copy(bf16[16,32,512]{2,1,0:T(8,128)(2,1)} %bitcast.5) | data formatting | bytes 1048576
  113.2 1.9 %copy.10 = bf16[16,32,512]{2,1,0:T(8,128)(2,1)} copy(bf16[16,32,512]{2,1,0:T(8,128)(2,1)} %bitcast.4) | data formatting | bytes 1048576

commit v4 on v3

--- a/solution.py
+++ b/solution.py
@@ -10,7 +10,7 @@
 F32 = jnp.float32
 NT = (((1,), (1,)), ((), ()))
 NN = (((1,), (0,)), ((), ()))
-N_STAGE = 13
+N_STAGE = 14
 N_COPIES = 500
 
 
@@ -19,7 +19,7 @@
 
 
 def kernel(wave, lops, rops, pat, sizes, out1, out2, *scratch):
-    wbuf, lf, rf, rsel, lsel, va, vb, mid, f1, f2, obuf, lsem, ssem, rsem, relay = scratch[: -2 * N_STAGE]
+    wbuf, lf, rf, rsel, lsel, va, vb, mid, f2, obuf, lsem, ssem, rsem, relay = scratch[: -2 * N_STAGE]
     stage1, stage2 = scratch[-2 * N_STAGE : -N_STAGE], scratch[-N_STAGE:]
     ops, sec = lax.axis_index("ops"), lax.axis_index("sec")
     x, zh, c = ops // 8, (ops // 2) % 4, ops % 2
@@ -39,7 +39,6 @@
     other = {"ops": ops + 1 - 2 * c, "sec": sec}
 
     sent = []
-    relayed = [2]
     count = [0]
 
     def copies(n):
@@ -161,10 +160,11 @@
         while sent:
             sent.pop().wait_send()
 
-    def reduce(pair, half, cut, finish, s0s, s0r, s0, r1y, r1x, t1, t2, t2b, r2x, r2y, wf, wb, r3):
-        p0, py, px, qx, qy, p3 = copies(4), copies(12), copies(6), copies(6), copies(6), copies(6)
-        for k, d in enumerate((1, 2, 3, 0)):
-            s0s[k] = pair(1 - c, (x + d) % 4).astype(BF)
+    def reduce(pair, half, finish, s0s, s0r, s0, r1y, r1x, t1, t2, t2b, r2x, r2y, wb, z1, sb, z2):
+        pair_z = 4 - 8 * (zh % 2)
+        p0, py, px, qx, qy, p3 = copies(4), copies(12), copies(6), copies(6), copies(6), copies(8)
+        def theirs(k):
+            s0s[k] = pair(1 - c, (x + k + 1) % 4).astype(BF)
             send(s0s.at[k], s0r.at[k], p0 + k, other)
 
         def first_sends(k, ch):
@@ -176,14 +176,21 @@
                     send(s0.at[pl.ds(k - 1, 2), ch, 0, q], r1y.at[ch, e - 1, pl.ds(k - 1, 2)],
                          py + 6 * ch + 3 * (k // 2) + e - 1, to_y(e))
 
-        for k, d in enumerate((1, 2, 3, 0)):
-            total = pair(c, (x + d) % 4)
+        def ours(k):
+            total = pair(c, (x + k + 1) % 4)
             arrived(s0r.at[k], p0 + k)
             total = total + s0r[k].astype(F32)
             for ch in range(2):
                 for bp in range(2):
                     s0[k, ch, bp] = total[bp, :, ch * half : (ch + 1) * half].astype(BF)
             first_sends(k, 0)
+
+        for k in (0, 1, 2):
+            theirs(k)
+        ours(0)
+        theirs(3)
+        for k in (1, 2, 3):
+            ours(k)
         for k in range(4):
             first_sends(k, 1)
 
@@ -213,28 +220,26 @@
                 send(t2b.at[ch, e - 1], r2y.at[ch, e - 1], qy + 3 * ch + e - 1, to_y(e))
             yield
             w0 = sum_t1(3)
-            w1 = t2[ch, y]
             for k in range(3):
                 arrived(r2x.at[ch, k], qx + 3 * ch + k)
                 w0 = w0 + r2x[ch, k].astype(F32)
+            wb[ch, 0] = w0.astype(BF)
+            send(wb.at[ch, 0], z1.at[ch, 0], p3 + 4 * ch, to_z(pair_z))
+            w1 = t2[ch, y]
             for k in range(3):
                 arrived(r2y.at[ch, k], qy + 3 * ch + k)
                 w1 = w1 + r2y[ch, k].astype(F32)
-            if relayed:
-                pl.semaphore_wait(relay.at[1], relayed.pop())
-            for bp, w in enumerate((w0, w1)):
-                for part in range(2):
-                    piece = cut(w, part)
-                    wf[ch, 2 * bp + part] = piece
-                    wb[ch, 2 * bp + part] = piece.astype(BF)
-            for d in (1, 3, 2):
-                send(wb.at[ch, (zh + d) % 4], r3.at[ch, d - 1], p3 + 3 * ch + d - 1, to_z(4 * d))
+            wb[ch, 1] = w1.astype(BF)
+            send(wb.at[ch, 1], z1.at[ch, 1], p3 + 4 * ch + 1, to_z(-pair_z))
             yield
-            total = wf[ch, zh]
-            for d in (1, 3, 2):
-                arrived(r3.at[ch, d - 1], p3 + 3 * ch + d - 1)
-                total = total + r3[ch, d - 1].astype(F32)
-            yield from finish(ch, total)
+            for bp, d in ((0, -pair_z), (1, pair_z)):
+                arrived(z1.at[ch, bp], p3 + 4 * ch + bp)
+                sb[ch, bp] = (wb[ch, bp].astype(F32) + z1[ch, bp].astype(F32)).astype(BF)
+                send(sb.at[ch, bp], z2.at[ch, bp], p3 + 4 * ch + 2 + bp, to_z(d))
+            yield
+            for bp in range(2):
+                arrived(z2.at[ch, bp], p3 + 4 * ch + 2 + bp)
+            yield from finish(ch, [sb[ch, bp].astype(F32) + z2[ch, bp].astype(F32) for bp in range(2)])
 
         return [flow(0), flow(1)]
 
@@ -244,6 +249,7 @@
         return jnp.where(k == m // 32 * 128 + y * 32 + m % 32, 1.0, 0.0).astype(BF)
 
     start = gather(va, None, True)
+    next(start)
     next(start)
     load_r.wait()
     load_l.wait()
@@ -251,7 +257,6 @@
     for t in range(3):
         rsel[pl.ds(128 * t, 128)] = dot(pick_t, rf[t], NT).astype(BF)
     next(start)
-    next(start)
 
     def left_half(cc):
         lrows = jnp.concatenate([lf[t, pl.ds(zl * 128, 128)] for t in range(3)], axis=0)
@@ -270,8 +275,6 @@
     next(start)
     left_half(1 - c)
     pl.semaphore_wait(relay.at[0], 2)
-    for d in (4, -4):
-        pl.semaphore_signal(relay.at[1], inc=1, device_id=to_z(d), device_id_type=MESH)
 
     def pair1(cc, xx):
         rows = []
@@ -281,31 +284,16 @@
         res = dot(jnp.concatenate(rows, axis=0), rsel[...], NN)
         return res.reshape(2, 4, 32, 512)
 
-    b_mine = c * 8 + x * 2 + zh // 2
-
-    def columns(part):
-        return pl.ds(pl.multiple_of(part * 256, 256), 256)
-
-    def finish1(ch, total):
-        rr = lax.broadcasted_iota(jnp.int32, (16, 256), 0) + (zl * 128 + y * 32 + 16 * ch)
-        cc_ = lax.broadcasted_iota(jnp.int32, (16, 256), 1) + zh % 2 * 256
-        f1[ch] = jnp.where(jnp.maximum(rr, cc_) < sizes[b_mine], total, 0.0).astype(BF)
-        here = vb.at[zl, c, x, ch, zh // 2, :, columns(zh % 2)]
-        own = pltpu.make_async_copy(f1.at[ch], here, lsem.at[3 + ch])
-        own.start()
-        g1 = copies(3)
-        for d in (1, 3, 2):
-            send(f1.at[ch], here, g1 + d - 1, to_z(4 * d))
-        yield
-        own.wait()
-        for d in (1, 3, 2):
-            h = (zh + 4 - d) % 4
-            arrived(vb.at[zl, c, x, ch, h // 2, :, columns(h % 2)], g1 + d - 1)
+    def finish1(ch, totals):
+        rr = lax.broadcasted_iota(jnp.int32, (16, 512), 0) + (zl * 128 + y * 32 + 16 * ch)
+        edge = jnp.maximum(rr, lax.broadcasted_iota(jnp.int32, (16, 512), 1))
+        for bp in range(2):
+            vb[zl, c, x, ch, bp] = jnp.where(edge < sizes[c * 8 + x * 2 + bp], totals[bp], 0.0).astype(BF)
         yield from gather(vb, ch, False)
 
-    flows = reduce(pair1, 16, lambda w, part: w[:, 256 * part : 256 * part + 256], finish1, *stage1)
+    flows = reduce(pair1, 16, finish1, *stage1)
     pick_n = pick((512, 128), 0)
-    run(flows, 1)
+    run(flows, 2)
     for t in range(3):
         chosen = dot(lf[t], pick_n, NN).astype(BF)
         for zz in range(4):
@@ -314,7 +302,7 @@
                     a = zz * 128 + q * 32 + rh * 16
                     b = q * 128 + rh * 64 + zz * 16
                     lsel[b : b + 16, 128 * t : 128 * t + 128] = chosen[a : a + 16]
-    run(flows, 5)
+    run(flows, 4)
 
     def right_half(cc):
         rrows = jnp.concatenate([rf[t, pl.ds(zl * 128, 128)] for t in range(3)], axis=0)
@@ -351,56 +339,26 @@
         res = dot(lsel[...], jnp.concatenate(cols, axis=1), NN)
         return jnp.stack([res[:, :128].reshape(4, 128, 128), res[:, 128:].reshape(4, 128, 128)])
 
-    def finish2(ch, total):
-        total = total.reshape(2, 16, 128)
-        shape = (2, 16, 128)
+    def lanes(zz):
+        return pl.ds(pl.multiple_of(zz * 128, 128), 128)
+
+    def finish2(ch, totals):
+        shape = (4, 16, 128)
         rr = lax.broadcasted_iota(jnp.int32, shape, 0) * 128 + lax.broadcasted_iota(jnp.int32, shape, 1)
-        rr = rr + (zh % 2 * 256 + y * 32 + 16 * ch)
-        cc_ = lax.broadcasted_iota(jnp.int32, shape, 2) + zl * 128
-        f2[ch] = jnp.where(jnp.maximum(rr, cc_) < sizes[b_mine], total, 0.0).astype(BF)
-        g2, out = copies(8), copies(8)
-        here = obuf.at[c, x, ch, zh // 2, :, pl.ds(pl.multiple_of(zl * 128, 128), 128)]
-        for i in range(2):
-            to = zh % 2 * 2 + i
-            for dh in (0, 1, 3, 2):
-                device = {"ops": (x * 4 + (zh + dh) % 4) * 2 + c, "sec": to * 4 + y}
-                if dh:
-                    send(f2.at[ch, i], here, g2 + 4 * (dh // 2) + zl, device, out + 4 * i + dh)
-                else:
-
-                    @pl.when(to != zl)
-                    def _():
-                        remote(f2.at[ch, i], here, g2 + zl, device, out + 4 * i).start()
-
-                    @pl.when(to == zl)
-                    def _():
-                        pltpu.make_async_copy(f2.at[ch, i], here, lsem.at[9 + ch]).start()
-
-        yield
-        for i in range(2):
-            to = zh % 2 * 2 + i
-
-            @pl.when(to != zl)
-            def _():
-                remote(f2.at[ch, i], here, g2 + zl, other, out + 4 * i).wait_send()
-
-            @pl.when(to == zl)
-            def _():
-                pltpu.make_async_copy(f2.at[ch, i], here, lsem.at[9 + ch]).wait()
-
-        odd = (zh + zl // 2) % 2
-        for j in range(2):
-            h = (zh + 4 - 2 * j - odd) % 4
-            for zz in range(4):
-                there = obuf.at[c, x, ch, h // 2, :, pl.ds(128 * zz, 128)]
-                if j:
-                    arrived(there, g2 + 4 + zz)
-                else:
-
-                    @pl.when((zz != zl) | (odd != 0))
-                    def _():
-                        arrived(there, g2 + zz)
-
+        edge = jnp.maximum(rr + (y * 32 + 16 * ch), lax.broadcasted_iota(jnp.int32, shape, 2) + zl * 128)
+        for bp in range(2):
+            f2[ch, bp] = jnp.where(edge < sizes[c * 8 + x * 2 + bp], totals[bp].reshape(shape), 0.0).astype(BF)
+        here = obuf.at[c, x, ch, :, :, lanes(zl)]
+        own = pltpu.make_async_copy(f2.at[ch, :, zl], here, lsem.at[3 + ch])
+        own.start()
+        g2 = copies(3)
+        away = (1, -1, 2 - 4 * ch)
+        for k, d in enumerate(away):
+            send(f2.at[ch, :, (zl + d + 4) % 4], here, g2 + k, to_z(d))
+        yield
+        own.wait()
+        for k, d in enumerate(away):
+            arrived(obuf.at[c, x, ch, :, :, lanes((zl - d + 4) % 4)], g2 + k)
         gx, gc = copies(3), copies(4)
         block = obuf.at[c, x, ch]
         for d in (1, 2, 3):
@@ -416,10 +374,10 @@
             arrived(obuf.at[1 - c, (x + 4 - d) % 4, ch], gc + d)
         yield
 
-    flows = reduce(pair2, 64, lambda w, part: w[32 * part : 32 * part + 32], finish2, *stage2)
+    flows = reduce(pair2, 64, finish2, *stage2)
     run(flows, 2)
     drain()
-    run(flows, 4)
+    run(flows, 5)
     store(obuf, out2, 11)
     drain()
     for cp in stores:
@@ -428,7 +386,7 @@
 
 
 def on_device(wave_t, left_ops, right_ops, pattern, sector_size):
-    def stage(r, w, piece):
+    def stage(r, w):
         return [
             pltpu.VMEM((4, 2, 4, 2 * r, w), BF),
             pltpu.VMEM((4, 2, 4, 2 * r, w), BF),
@@ -440,9 +398,10 @@
             pltpu.VMEM((2, 3, r, w), BF),
             pltpu.VMEM((2, 3, r, w), BF),
             pltpu.VMEM((2, 3, r, w), BF),
-            pltpu.VMEM((2, 4, *piece), F32),
-            pltpu.VMEM((2, 4, *piece), BF),
-            pltpu.VMEM((2, 3, *piece), BF),
+            pltpu.VMEM((2, 2, r, w), BF),
+            pltpu.VMEM((2, 2, r, w), BF),
+            pltpu.VMEM((2, 2, r, w), BF),
+            pltpu.VMEM((2, 2, r, w), BF),
         ]
 
     hbm = pl.BlockSpec(memory_space=pl.ANY)
@@ -462,15 +421,14 @@
             pltpu.VMEM((4, 2, 4, 2, 2, 16, 512), BF),
             pltpu.VMEM((4, 2, 4, 2, 2, 16, 512), BF),
             pltpu.VMEM((3, 16, 128, 128), BF),
-            pltpu.VMEM((2, 16, 256), BF),
-            pltpu.VMEM((2, 2, 16, 128), BF),
+            pltpu.VMEM((2, 2, 4, 16, 128), BF),
             pltpu.VMEM((2, 4, 2, 2, 16, 512), BF),
             pltpu.SemaphoreType.DMA((16,)),
             pltpu.SemaphoreType.DMA((N_COPIES,)),
             pltpu.SemaphoreType.DMA((N_COPIES,)),
-            pltpu.SemaphoreType.REGULAR((2,)),
-            *stage(16, 512, (16, 256)),
-            *stage(64, 128, (32, 128)),
+            pltpu.SemaphoreType.REGULAR((1,)),
+            *stage(16, 512),
+            *stage(64, 128),
         ],
         compiler_params=pltpu.CompilerParams(
             collective_id=0, has_side_effects=True, vmem_limit_bytes=58 * 2**20

time: 115 us -> 112 us (0.974)
  Pallas kernels: 111 us -> 107 us
    pallas_call x1, Pallas kernels: 111 us -> 107 us  [on_device(): pl.pallas_call(kernel, out_shape=(out, out), in_specs=[hbm, hbm, hbm, sme...]
where the time goes in v4:
time: 112 us; the launch traced here: 111 us
  Pallas kernels  107 us (96%)
  local copies, waits for them, and re-layouts  3.76 us (3%)
    pallas_call x1, Pallas kernels, on_device(): pl.pallas_call(kernel, out_shape=(out, out), in_specs=[hbm, hbm, hbm, sme...  107 us
    unnamed x2, local copies, waits for them, and re-layouts  3.76 us

profile of v4, /device:TPU:1, one launch (start us, length us, event | category | flops | bytes accessed | tf_op | source)
XLA Modules:
  0.0 111.3 jit_solution(2305303840310831)
XLA Ops:
  0.6 106.9 %hamiltonian.1 = (bf16[2,4,2,2,16,512]{5,4,3,2,1,0:T(8,128)(2,1)}, bf16[2,4,2,2,16,512]{5,4,3,2,1,0:T(8,128)(2,1)}) custom-call(bf16[2,4,2,2,16,512]{5,4,3,2,1,0:T(8,128)(2,1)} %bitcast.3, bf16[3,512,512]{2,1,0:T(8,128)(2,1)} %lops.1, bf16[3,512,512]{2,1,0:T(8,128)(2,1)} %rops.1, s32[3,16]{1,0:T(4,128)} %pat.1, s32[16]{0:T(128)} %sizes.1), custom_call_target="tpu_custom_call" | custom-call | tf_op jit(solution)/shard_map/hamiltonian/pallas_call | solution.py:410
  107.6 1.9 %copy.9 = bf16[16,32,512]{2,1,0:T(8,128)(2,1)} copy(bf16[16,32,512]{2,1,0:T(8,128)(2,1)} %bitcast.5) | data formatting | bytes 1048576
  109.5 1.9 %copy.10 = bf16[16,32,512]{2,1,0:T(8,128)(2,1)} copy(bf16[16,32,512]{2,1,0:T(8,128)(2,1)} %bitcast.4) | data formatting | bytes 1048576

commit v5 on v4

--- a/solution.py
+++ b/solution.py
@@ -11,7 +11,8 @@
 NT = (((1,), (1,)), ((), ()))
 NN = (((1,), (0,)), ((), ()))
 N_STAGE = 14
-N_COPIES = 500
+N_ARRIVALS = 106
+N_SENDS = 56
 
 
 def dot(a, b, dims):
@@ -46,16 +47,22 @@
         count[0] += n
         return first
 
-    def remote(src, dst, index, device, out_index=None):
-        return pltpu.make_async_remote_copy(
-            src_ref=src, dst_ref=dst, send_sem=ssem.at[index if out_index is None else out_index], recv_sem=rsem.at[index],
-            device_id=device, device_id_type=MESH,
-        )
-
-    def send(src, dst, index, device, out_index=None):
-        cp = remote(src, dst, index, device, out_index)
-        cp.start()
-        sent.append(cp)
+    def send_all(group, total):
+        i = len(sent)
+        assert i < N_SENDS, i
+        for src, dst, index, device in group:
+            pltpu.make_async_remote_copy(
+                src_ref=src, dst_ref=dst, send_sem=ssem.at[i], recv_sem=rsem.at[index],
+                device_id=device, device_id_type=MESH,
+            ).start()
+        sent.append(pltpu.make_async_copy(total, total, ssem.at[i]))
+
+    def send(src, dst, index, device):
+        send_all([(src, dst, index, device)], src)
+
+    def drain():
+        while sent:
+            sent.pop().wait()
 
     def arrived(ref, index):
         pltpu.make_async_copy(ref, ref, rsem.at[index]).wait()
@@ -96,15 +103,15 @@
     def gather(v, chunk, whole_slab):
         halves = (0, 1) if chunk is None else (chunk,)
         rows = pl.ds(halves[0], len(halves))
-        a1, b1, a2, b2, cx = copies(4), copies(3), copies(12), copies(16), copies(4)
+        a1, b1, a2, b2, cx = copies(4), copies(3), copies(4), copies(4), copies(1)
 
         def z_send(xx, bp, i0):
             block = v.at[zl, c, xx, rows, bp]
-            send(block, block, i0, to_z(1))
-            send(block, block, i0 + 1, to_z(-1))
+            group = [(block, block, i0, to_z(1)), (block, block, i0 + 1, to_z(-1))]
             for rh in halves:
-                block = v.at[zl, c, xx, rh, bp]
-                send(block, block, i0 + 2 + rh, to_z(2 - 4 * rh))
+                part = v.at[zl, c, xx, rh, bp]
+                group.append((part, part, i0 + 2 + rh, to_z(2 - 4 * rh)))
+            send_all(group, v.at[zl, c, pl.ds(0, 3), rows, bp])
 
         def z_arrived(xx, bp, k, i0):
             if k < 3:
@@ -113,42 +120,37 @@
                 for rh in halves:
                     arrived(v.at[z_of[k], c, xx, rh, bp], i0 + 2 + rh)
 
-        def x_send(zz, bp, i0):
+        def x_send(zz, bp, indices):
             block = v.at[zz, c, x, rows, bp]
-            for d in (1, 2, 3):
-                send(block, block, i0 + d - 1, to_x(d))
+            group = [(block, block, i, to_x(d)) for d, i in zip((1, 2, 3), indices)]
+            send_all(group, v.at[zz, c, pl.ds(0, 3), rows, bp])
 
         z_send(x, 0, a1)
         if whole_slab:
             for k in range(4):
-                z_send(x_of[k], 1, b2 + 4 * k)
+                z_send(x_of[k], 1, b2)
         else:
-            x_send(zl, 1, b1)
-            x_send(zl, 0, a2)
+            x_send(zl, 1, (b1, b1 + 1, b1 + 2))
+            x_send(zl, 0, (a2, a2, a2))
             z_send(x, 1, b2)
         yield
         for k in (1, 2, 3):
             if not whole_slab:
                 arrived(v.at[zl, c, x_of[k], rows, 1], b1 + step[k] - 1)
-                z_send(x_of[k], 1, b2 + 4 * k)
+                z_send(x_of[k], 1, b2)
             z_arrived(x, 0, k, a1)
-            x_send(z_of[k], 0, a2 + 3 * k)
+            x_send(z_of[k], 0, (a2 + k, a2 + k, a2 + k))
         yield
         for k in range(4):
             if k == 0 and whole_slab:
                 continue
-            for m in (1, 2, 3):
-                arrived(v.at[z_of[k], c, x_of[m], rows, 0], a2 + 3 * k + step[m] - 1)
+            arrived(v.at[z_of[k], c, pl.ds(0, 3), rows, 0], a2 + k)
             if k > 0:
-                for m in range(4):
-                    z_arrived(x_of[m], 1, k, b2 + 4 * m)
+                z_arrived(slice(None), 1, k, b2)
             block = v.at[z_of[k], c, :, rows]
-            send(block, block, cx + k, other)
-        yield
-        for k in range(4):
-            if k == 0 and whole_slab:
-                continue
-            arrived(v.at[z_of[k], 1 - c, :, rows], cx + k)
+            send(block, block, cx, other)
+        yield
+        arrived(v.at[pl.ds(0, 3 if whole_slab else 4), 1 - c, :, rows], cx)
         yield
 
     def run(flows, steps):
@@ -156,25 +158,22 @@
             for flow in flows:
                 next(flow)
 
-    def drain():
-        while sent:
-            sent.pop().wait_send()
-
     def reduce(pair, half, finish, s0s, s0r, s0, r1y, r1x, t1, t2, t2b, r2x, r2y, wb, z1, sb, z2):
         pair_z = 4 - 8 * (zh % 2)
-        p0, py, px, qx, qy, p3 = copies(4), copies(12), copies(6), copies(6), copies(6), copies(8)
+        p0, py, px, qx, qy, p3 = copies(4), copies(4), copies(2), copies(2), copies(2), copies(8)
         def theirs(k):
             s0s[k] = pair(1 - c, (x + k + 1) % 4).astype(BF)
             send(s0s.at[k], s0r.at[k], p0 + k, other)
 
         def first_sends(k, ch):
             if k < 3:
-                send(s0.at[k, ch, 1], r1x.at[ch, k], px + 3 * ch + k, to_x(k + 1))
+                send(s0.at[k, ch, 1], r1x.at[ch, k], px + ch, to_x(k + 1))
             if k % 2:
-                for e in (1, 2, 3):
-                    q = (y + e) % 4
-                    send(s0.at[pl.ds(k - 1, 2), ch, 0, q], r1y.at[ch, e - 1, pl.ds(k - 1, 2)],
-                         py + 6 * ch + 3 * (k // 2) + e - 1, to_y(e))
+                two = pl.ds(k - 1, 2)
+                group = [
+                    (s0.at[two, ch, 0, (y + e) % 4], r1y.at[ch, e - 1, two], py + 2 * ch + k // 2, to_y(e)) for e in (1, 2, 3)
+                ]
+                send_all(group, r1y.at[ch, :, two])
 
         def ours(k):
             total = pair(c, (x + k + 1) % 4)
@@ -203,13 +202,13 @@
 
             for k in range(4):
                 if k % 2 == 0:
-                    for e in (1, 2, 3):
-                        arrived(r1y.at[ch, e - 1, pl.ds(k, 2)], py + 6 * ch + 3 * (k // 2) + e - 1)
+                    arrived(r1y.at[ch, :, pl.ds(k, 2)], py + 2 * ch + k // 2)
                 if k < 3:
                     t1[ch, k] = sum_t1(k).astype(BF)
-                    send(t1.at[ch, k], r2x.at[ch, k], qx + 3 * ch + k, to_x(k + 1))
-            for k in range(3):
-                arrived(r1x.at[ch, k], px + 3 * ch + k)
+                    if k == 2:
+                        group = [(t1.at[ch, m], r2x.at[ch, m], qx + ch, to_x(m + 1)) for m in range(3)]
+                        send_all(group, r2x.at[ch])
+            arrived(r1x.at[ch], px + ch)
             mine = s0[3, ch, 1].astype(F32)
             for k in range(3):
                 mine = mine + r1x[ch, k].astype(F32)
@@ -217,17 +216,18 @@
             for e in (1, 2, 3):
                 q = (y + e) % 4
                 t2b[ch, e - 1] = t2[ch, q].astype(BF)
-                send(t2b.at[ch, e - 1], r2y.at[ch, e - 1], qy + 3 * ch + e - 1, to_y(e))
+            group = [(t2b.at[ch, e - 1], r2y.at[ch, e - 1], qy + ch, to_y(e)) for e in (1, 2, 3)]
+            send_all(group, r2y.at[ch])
             yield
             w0 = sum_t1(3)
+            arrived(r2x.at[ch], qx + ch)
             for k in range(3):
-                arrived(r2x.at[ch, k], qx + 3 * ch + k)
                 w0 = w0 + r2x[ch, k].astype(F32)
             wb[ch, 0] = w0.astype(BF)
             send(wb.at[ch, 0], z1.at[ch, 0], p3 + 4 * ch, to_z(pair_z))
             w1 = t2[ch, y]
+            arrived(r2y.at[ch], qy + ch)
             for k in range(3):
-                arrived(r2y.at[ch, k], qy + 3 * ch + k)
                 w1 = w1 + r2y[ch, k].astype(F32)
             wb[ch, 1] = w1.astype(BF)
             send(wb.at[ch, 1], z1.at[ch, 1], p3 + 4 * ch + 1, to_z(-pair_z))
@@ -294,6 +294,7 @@
     flows = reduce(pair1, 16, finish1, *stage1)
     pick_n = pick((512, 128), 0)
     run(flows, 2)
+    drain()
     for t in range(3):
         chosen = dot(lf[t], pick_n, NN).astype(BF)
         for zz in range(4):
@@ -359,19 +360,17 @@
         own.wait()
         for k, d in enumerate(away):
             arrived(obuf.at[c, x, ch, :, :, lanes((zl - d + 4) % 4)], g2 + k)
-        gx, gc = copies(3), copies(4)
+        gx, gc = copies(3), copies(1)
         block = obuf.at[c, x, ch]
-        for d in (1, 2, 3):
-            send(block, block, gx + d - 1, to_x(d))
+        send_all([(block, block, gx + d - 1, to_x(d)) for d in (1, 2, 3)], obuf.at[c, pl.ds(0, 3), ch])
         send(block, block, gc, other)
         yield
         for d in (1, 3, 2):
             block = obuf.at[c, (x + 4 - d) % 4, ch]
             arrived(block, gx + d - 1)
-            send(block, block, gc + d, other)
-        yield
-        for d in range(4):
-            arrived(obuf.at[1 - c, (x + 4 - d) % 4, ch], gc + d)
+            send(block, block, gc, other)
+        yield
+        arrived(obuf.at[1 - c, :, ch], gc)
         yield
 
     flows = reduce(pair2, 64, finish2, *stage2)
@@ -382,7 +381,20 @@
     drain()
     for cp in stores:
         cp.wait()
-    assert count[0] <= N_COPIES, count
+    assert count[0] == N_ARRIVALS, count
+
+
+def hand_over(first, second, out1, out2, sem):
+    cps = []
+    for i, (src, dst) in enumerate(((first, out1), (second, out2))):
+        for cc in range(2):
+            for part in range(2):
+                where = (cc, pl.ds(2 * part, 2))
+                cps.append(pltpu.make_async_copy(src.at[where], dst.at[where], sem.at[4 * i + 2 * cc + part]))
+    for cp in cps:
+        cp.start()
+    for cp in cps:
+        cp.wait()
 
 
 def on_device(wave_t, left_ops, right_ops, pattern, sector_size):
@@ -424,8 +436,8 @@
             pltpu.VMEM((2, 2, 4, 16, 128), BF),
             pltpu.VMEM((2, 4, 2, 2, 16, 512), BF),
             pltpu.SemaphoreType.DMA((16,)),
-            pltpu.SemaphoreType.DMA((N_COPIES,)),
-            pltpu.SemaphoreType.DMA((N_COPIES,)),
+            pltpu.SemaphoreType.DMA((N_SENDS,)),
+            pltpu.SemaphoreType.DMA((N_ARRIVALS,)),
             pltpu.SemaphoreType.REGULAR((1,)),
             *stage(16, 512),
             *stage(64, 128),
@@ -435,6 +447,14 @@
         ),
         name="hamiltonian",
     )(wave_t.reshape(2, 4, 2, 2, 16, 512), left_ops, right_ops, pattern, sector_size)
+    first, second = pl.pallas_call(
+        hand_over,
+        out_shape=(out, out),
+        in_specs=[hbm, hbm],
+        out_specs=(hbm, hbm),
+        scratch_shapes=[pltpu.SemaphoreType.DMA((8,))],
+        name="hand_over",
+    )(first, second)
     return first.reshape(16, 32, 512), second.reshape(16, 32, 512)
 
 

time: 112 us -> 134 us (1.20)
  Pallas kernels: 107 us -> 133 us
  local copies, waits for them, and re-layouts: 3.76 us -> 0 us
    pallas_call x0 -> x1, Pallas kernels: none -> 32.9 us  [on_device(): pl.pallas_call(hand_over, out_shape=(out, out), in_specs=[hbm, hbm], out_...]
    pallas_call x1, Pallas kernels: 107 us -> 100 us  [on_device(): pl.pallas_call(kernel, out_shape=(out, out), in_specs=[hbm, hbm, hbm, sme...]
    unnamed x2 -> x0, local copies, waits for them, and re-layouts: 3.76 us -> none
where the time goes in v5:
time: 134 us
  Pallas kernels  133 us (99%)
    pallas_call x1, Pallas kernels, on_device(): pl.pallas_call(kernel, out_shape=(out, out), in_specs=[hbm, hbm, hbm, sme...  100 us
    pallas_call x1, Pallas kernels, on_device(): pl.pallas_call(hand_over, out_shape=(out, out), in_specs=[hbm, hbm], out_...  32.9 us

profile of v5, /device:TPU:1, one launch (start us, length us, event | category | flops | bytes accessed | tf_op | source)
XLA Modules:
  0.0 133.8 jit_solution(7208632393336887158)
XLA Ops:
  0.6 100.2 %hamiltonian.1 = (bf16[2,4,2,2,16,512]{5,4,3,2,1,0:T(8,128)(2,1)}, bf16[2,4,2,2,16,512]{5,4,3,2,1,0:T(8,128)(2,1)}) custom-call(bf16[2,4,2,2,16,512]{5,4,3,2,1,0:T(8,128)(2,1)} %bitcast.3, bf16[3,512,512]{2,1,0:T(8,128)(2,1)} %lops.1, bf16[3,512,512]{2,1,0:T(8,128)(2,1)} %rops.1, s32[3,16]{1,0:T(4,128)} %pat.1, s32[16]{0:T(128)} %sizes.1), custom_call_target="tpu_custom_call" | custom-call | tf_op jit(solution)/shard_map/hamiltonian/pallas_call | solution.py:422
  100.9 32.9 %hand_over.1 = (bf16[2,4,2,2,16,512]{5,4,3,2,1,0:T(8,128)(2,1)}, bf16[2,4,2,2,16,512]{5,4,3,2,1,0:T(8,128)(2,1)}) custom-call(bf16[2,4,2,2,16,512]{5,4,3,2,1,0:T(8,128)(2,1)} %get-tuple-element.6.first, bf16[2,4,2,2,16,512]{5,4,3,2,1,0:T(8,128)(2,1)} %get-tuple-element.7.second), custom_call_target="tpu_custom_call" | custom-call | tf_op jit(solution)/shard_map/hand_over/pallas_call | solution.py:450

commit v6 on v5

--- a/solution.py
+++ b/solution.py
@@ -384,17 +384,19 @@
     assert count[0] == N_ARRIVALS, count
 
 
-def hand_over(first, second, out1, out2, sem):
-    cps = []
+def hand_over(first, second, out1, out2, held, sem):
+    steps = []
     for i, (src, dst) in enumerate(((first, out1), (second, out2))):
-        for cc in range(2):
-            for part in range(2):
-                where = (cc, pl.ds(2 * part, 2))
-                cps.append(pltpu.make_async_copy(src.at[where], dst.at[where], sem.at[4 * i + 2 * cc + part]))
-    for cp in cps:
-        cp.start()
-    for cp in cps:
-        cp.wait()
+        for k in range(4):
+            part = pl.ds(4 * k, 4)
+            load = pltpu.make_async_copy(src.at[part], held.at[i, part], sem.at[i, k, 0])
+            load.start()
+            steps.append((load, pltpu.make_async_copy(held.at[i, part], dst.at[part], sem.at[i, k, 1])))
+    for load, store in steps:
+        load.wait()
+        store.start()
+    for _, store in steps:
+        store.wait()
 
 
 def on_device(wave_t, left_ops, right_ops, pattern, sector_size):
@@ -447,15 +449,16 @@
         ),
         name="hamiltonian",
     )(wave_t.reshape(2, 4, 2, 2, 16, 512), left_ops, right_ops, pattern, sector_size)
-    first, second = pl.pallas_call(
+    result = jax.ShapeDtypeStruct((16, 32, 512), BF)
+    return pl.pallas_call(
         hand_over,
-        out_shape=(out, out),
+        out_shape=(result, result),
         in_specs=[hbm, hbm],
         out_specs=(hbm, hbm),
-        scratch_shapes=[pltpu.SemaphoreType.DMA((8,))],
+        scratch_shapes=[pltpu.VMEM((2, 16, 32, 512), BF), pltpu.SemaphoreType.DMA((2, 4, 2))],
+        compiler_params=pltpu.CompilerParams(vmem_limit_bytes=58 * 2**20),
         name="hand_over",
-    )(first, second)
-    return first.reshape(16, 32, 512), second.reshape(16, 32, 512)
+    )(first.reshape(16, 32, 512), second.reshape(16, 32, 512))
 
 
 def solution(mesh):

time: 134 us -> 103 us (0.77)
  Pallas kernels: 133 us -> 102 us
    pallas_call x1, Pallas kernels: 32.9 us -> 2.09 us  [on_device(): pl.pallas_call(hand_over, out_shape=(result, result), in_specs=[hbm, hbm]...]
where the time goes in v6:
time: 103 us
  Pallas kernels  102 us (99%)
    pallas_call x1, Pallas kernels, on_device(): pl.pallas_call(kernel, out_shape=(out, out), in_specs=[hbm, hbm, hbm, sme...  100 us
    pallas_call x1, Pallas kernels, on_device(): pl.pallas_call(hand_over, out_shape=(result, result), in_specs=[hbm, hbm]...  2.09 us

profile of v6, /device:TPU:1, one launch (start us, length us, event | category | flops | bytes accessed | tf_op | source)
XLA Modules:
  0.0 103.0 jit_solution(12883327931611572007)
XLA Ops:
  0.6 100.2 %hamiltonian.1 = (bf16[2,4,2,2,16,512]{5,4,3,2,1,0:T(8,128)(2,1)}, bf16[2,4,2,2,16,512]{5,4,3,2,1,0:T(8,128)(2,1)}) custom-call(bf16[2,4,2,2,16,512]{5,4,3,2,1,0:T(8,128)(2,1)} %bitcast.3, bf16[3,512,512]{2,1,0:T(8,128)(2,1)} %lops.1, bf16[3,512,512]{2,1,0:T(8,128)(2,1)} %rops.1, s32[3,16]{1,0:T(4,128)} %pat.1, s32[16]{0:T(128)} %sizes.1), custom_call_target="tpu_custom_call" | custom-call | tf_op jit(solution)/shard_map/hamiltonian/pallas_call | solution.py:424
  100.9 2.1 %hand_over.1 = (bf16[16,32,512]{2,1,0:T(8,128)(2,1)}, bf16[16,32,512]{2,1,0:T(8,128)(2,1)}) custom-call(bf16[16,32,512]{2,1,0:T(8,128)(2,1)} %bitcast.4, bf16[16,32,512]{2,1,0:T(8,128)(2,1)} %bitcast.5), custom_call_target="tpu_custom_call" | custom-call | tf_op jit(solution)/shard_map/hand_over/pallas_call | solution.py:453

commit v7 on v6

--- a/solution.py
+++ b/solution.py
@@ -11,8 +11,8 @@
 NT = (((1,), (1,)), ((), ()))
 NN = (((1,), (0,)), ((), ()))
 N_STAGE = 14
-N_ARRIVALS = 106
-N_SENDS = 56
+N_ARRIVALS = 99
+N_SENDS = 60
 
 
 def dot(a, b, dims):
@@ -36,6 +36,10 @@
     def to_z(d):
         w = (z + d + 16) % 16
         return {"ops": (x * 4 + w // 4) * 2 + c, "sec": w % 4 * 4 + y}
+
+    def to_xz(dx, d):
+        w = (z + d + 16) % 16
+        return {"ops": ((x + dx) % 4 * 4 + w // 4) * 2 + c, "sec": w % 4 * 4 + y}
 
     other = {"ops": ops + 1 - 2 * c, "sec": sec}
 
@@ -103,7 +107,7 @@
     def gather(v, chunk, whole_slab):
         halves = (0, 1) if chunk is None else (chunk,)
         rows = pl.ds(halves[0], len(halves))
-        a1, b1, a2, b2, cx = copies(4), copies(3), copies(4), copies(4), copies(1)
+        a1, b1, a2, b2, cx = copies(4), copies(3), copies(4), copies(4), copies(2)
 
         def z_send(xx, bp, i0):
             block = v.at[zl, c, xx, rows, bp]
@@ -141,16 +145,29 @@
             z_arrived(x, 0, k, a1)
             x_send(z_of[k], 0, (a2 + k, a2 + k, a2 + k))
         yield
+        if whole_slab:
+            for k in (1, 2, 3):
+                z_arrived(slice(None), 1, k, b2)
+                block = v.at[z_of[k], c, :, :, 1]
+                send(block, block, cx, other)
+            yield
+            for k in (1, 2, 3):
+                arrived(v.at[z_of[k], c, pl.ds(0, 3), rows, 0], a2 + k)
+                block = v.at[z_of[k], c, :, :, 0]
+                send(block, block, cx + 1, other)
+            yield
+            for i in range(2):
+                arrived(v.at[pl.ds(0, 3), 1 - c, :, :, 0], cx + i)
+                yield
+            return
         for k in range(4):
-            if k == 0 and whole_slab:
-                continue
             arrived(v.at[z_of[k], c, pl.ds(0, 3), rows, 0], a2 + k)
             if k > 0:
                 z_arrived(slice(None), 1, k, b2)
             block = v.at[z_of[k], c, :, rows]
             send(block, block, cx, other)
         yield
-        arrived(v.at[pl.ds(0, 3 if whole_slab else 4), 1 - c, :, rows], cx)
+        arrived(v.at[:, 1 - c, :, rows], cx)
         yield
 
     def run(flows, steps):
@@ -258,29 +275,34 @@
         rsel[pl.ds(128 * t, 128)] = dot(pick_t, rf[t], NT).astype(BF)
     next(start)
 
-    def left_half(cc):
+    def left_part(cc, bp):
         lrows = jnp.concatenate([lf[t, pl.ds(zl * 128, 128)] for t in range(3)], axis=0)
 
-        def body(xx, carry):
-            src = [va[:, cc, xx, :, bp].reshape(128, 512) for bp in range(2)]
+        def body(k, carry):
+            src = [va[:, cc, 2 * k + i, :, bp].reshape(128, 512) for i in range(2)]
             res = dot(lrows, jnp.concatenate(src, axis=0), NT).astype(BF)
             for t in range(3):
-                for bp in range(2):
-                    mid[t, cc * 8 + xx * 2 + bp] = res[128 * t : 128 * t + 128, 128 * bp : 128 * bp + 128]
+                for i in range(2):
+                    block = res[128 * t : 128 * t + 128, 128 * i : 128 * i + 128]
+                    mid[t, cc * 8 + (2 * k + i) * 2 + bp] = block.reshape(4, 2, 16, 128)
             return carry
 
-        lax.fori_loop(0, 4, body, 0)
-
-    left_half(c)
-    next(start)
-    left_half(1 - c)
+        lax.fori_loop(0, 2, body, 0)
+
+    left_part(c, 1)
+    next(start)
+    left_part(c, 0)
+    next(start)
+    left_part(1 - c, 1)
+    next(start)
+    left_part(1 - c, 0)
     pl.semaphore_wait(relay.at[0], 2)
 
     def pair1(cc, xx):
         rows = []
         for bp in range(2):
             b = cc * 8 + xx * 2 + bp
-            rows.append(jnp.concatenate([mid[t, pat[t, b]] for t in range(3)], axis=1))
+            rows.append(jnp.concatenate([mid[t, pat[t, b]].reshape(128, 128) for t in range(3)], axis=1))
         res = dot(jnp.concatenate(rows, axis=0), rsel[...], NN)
         return res.reshape(2, 4, 32, 512)
 
@@ -303,23 +325,20 @@
                     a = zz * 128 + q * 32 + rh * 16
                     b = q * 128 + rh * 64 + zz * 16
                     lsel[b : b + 16, 128 * t : 128 * t + 128] = chosen[a : a + 16]
-    run(flows, 4)
-
-    def right_half(cc):
+    run(flows, 3)
+
+    def right_part(cc, ch):
         rrows = jnp.concatenate([rf[t, pl.ds(zl * 128, 128)] for t in range(3)], axis=0)
-
-        def body(xx, carry):
-            src = [vb[:, cc, xx, :, bp].reshape(128, 512) for bp in range(2)]
-            res = dot(jnp.concatenate(src, axis=0), rrows, NT).astype(BF)
-            for t in range(3):
-                for bp in range(2):
-                    mid[t, cc * 8 + xx * 2 + bp] = res[128 * bp : 128 * bp + 128, 128 * t : 128 * t + 128]
-            return carry
-
-        lax.fori_loop(0, 4, body, 0)
-
-    right_half(c)
-    run(flows, 1)
+        res = dot(vb[:, cc, :, ch].reshape(512, 512), rrows, NT).astype(BF).reshape(4, 8, 16, 384)
+        for t in range(3):
+            for zz in range(4):
+                mid[t, pl.ds(cc * 8, 8), zz, ch] = res[zz, :, :, 128 * t : 128 * t + 128]
+
+    for ch in range(2):
+        next(flows[ch])
+        right_part(c, ch)
+        next(flows[ch])
+        right_part(1 - c, ch)
     stores = []
 
     def store(src, dst, index):
@@ -330,13 +349,12 @@
                 stores.append(cp)
 
     store(vb.at[zl], out1, 5)
-    right_half(1 - c)
 
     def pair2(cc, xx):
         cols = []
         for bp in range(2):
             b = cc * 8 + xx * 2 + bp
-            cols.append(jnp.concatenate([mid[t, pat[t, b]] for t in range(3)], axis=0))
+            cols.append(jnp.concatenate([mid[t, pat[t, b]].reshape(128, 128) for t in range(3)], axis=0))
         res = dot(lsel[...], jnp.concatenate(cols, axis=1), NN)
         return jnp.stack([res[:, :128].reshape(4, 128, 128), res[:, 128:].reshape(4, 128, 128)])
 
@@ -350,25 +368,15 @@
         for bp in range(2):
             f2[ch, bp] = jnp.where(edge < sizes[c * 8 + x * 2 + bp], totals[bp].reshape(shape), 0.0).astype(BF)
         here = obuf.at[c, x, ch, :, :, lanes(zl)]
-        own = pltpu.make_async_copy(f2.at[ch, :, zl], here, lsem.at[3 + ch])
-        own.start()
-        g2 = copies(3)
-        away = (1, -1, 2 - 4 * ch)
-        for k, d in enumerate(away):
-            send(f2.at[ch, :, (zl + d + 4) % 4], here, g2 + k, to_z(d))
-        yield
-        own.wait()
-        for k, d in enumerate(away):
-            arrived(obuf.at[c, x, ch, :, :, lanes((zl - d + 4) % 4)], g2 + k)
-        gx, gc = copies(3), copies(1)
-        block = obuf.at[c, x, ch]
-        send_all([(block, block, gx + d - 1, to_x(d)) for d in (1, 2, 3)], obuf.at[c, pl.ds(0, 3), ch])
+        g2, gc = copies(1), copies(1)
+        pltpu.make_async_copy(f2.at[ch, :, zl], here, rsem.at[g2]).start()
+        for d in (0, 1, -1, 2 - 4 * ch):
+            group = [(f2.at[ch, :, (zl + d + 4) % 4], here, g2, to_xz(dx, d)) for dx in (0, 1, 3, 2) if d or dx]
+            send_all(group, f2.at[ch, :, pl.ds(0, len(group))])
+        yield
+        block = obuf.at[c, :, ch]
+        arrived(block, g2)
         send(block, block, gc, other)
-        yield
-        for d in (1, 3, 2):
-            block = obuf.at[c, (x + 4 - d) % 4, ch]
-            arrived(block, gx + d - 1)
-            send(block, block, gc, other)
         yield
         arrived(obuf.at[1 - c, :, ch], gc)
         yield
@@ -376,7 +384,7 @@
     flows = reduce(pair2, 64, finish2, *stage2)
     run(flows, 2)
     drain()
-    run(flows, 5)
+    run(flows, 4)
     store(obuf, out2, 11)
     drain()
     for cp in stores:
@@ -434,7 +442,7 @@
             pltpu.VMEM((512, 384), BF),
             pltpu.VMEM((4, 2, 4, 2, 2, 16, 512), BF),
             pltpu.VMEM((4, 2, 4, 2, 2, 16, 512), BF),
-            pltpu.VMEM((3, 16, 128, 128), BF),
+            pltpu.VMEM((3, 16, 4, 2, 16, 128), BF),
             pltpu.VMEM((2, 2, 4, 16, 128), BF),
             pltpu.VMEM((2, 4, 2, 2, 16, 512), BF),
             pltpu.SemaphoreType.DMA((16,)),

time: 103 us -> 99.2 us (0.963)
  Pallas kernels: 102 us -> 98.4 us
    pallas_call x1, Pallas kernels: 100 us -> 96.3 us  [on_device(): pl.pallas_call(kernel, out_shape=(out, out), in_specs=[hbm, hbm, hbm, sme...]
where the time goes in v7:
time: 99.2 us; the launch traced here: 99 us
  Pallas kernels  98.4 us (99%)
    pallas_call x1, Pallas kernels, on_device(): pl.pallas_call(kernel, out_shape=(out, out), in_specs=[hbm, hbm, hbm, sme...  96.3 us
    pallas_call x1, Pallas kernels, on_device(): pl.pallas_call(hand_over, out_shape=(result, result), in_specs=[hbm, hbm]...  2.09 us

profile of v7, /device:TPU:1, one launch (start us, length us, event | category | flops | bytes accessed | tf_op | source)
XLA Modules:
  0.0 99.0 jit_solution(16692251662866121414)
XLA Ops:
  0.6 96.3 %hamiltonian.1 = (bf16[2,4,2,2,16,512]{5,4,3,2,1,0:T(8,128)(2,1)}, bf16[2,4,2,2,16,512]{5,4,3,2,1,0:T(8,128)(2,1)}) custom-call(bf16[2,4,2,2,16,512]{5,4,3,2,1,0:T(8,128)(2,1)} %bitcast.3, bf16[3,512,512]{2,1,0:T(8,128)(2,1)} %lops.1, bf16[3,512,512]{2,1,0:T(8,128)(2,1)} %rops.1, s32[3,16]{1,0:T(4,128)} %pat.1, s32[16]{0:T(128)} %sizes.1), custom_call_target="tpu_custom_call" | custom-call | tf_op jit(solution)/shard_map/hamiltonian/pallas_call | solution.py:432
  96.9 2.1 %hand_over.1 = (bf16[16,32,512]{2,1,0:T(8,128)(2,1)}, bf16[16,32,512]{2,1,0:T(8,128)(2,1)}) custom-call(bf16[16,32,512]{2,1,0:T(8,128)(2,1)} %bitcast.4, bf16[16,32,512]{2,1,0:T(8,128)(2,1)} %bitcast.5), custom_call_target="tpu_custom_call" | custom-call | tf_op jit(solution)/shard_map/hand_over/pallas_call | solution.py:461

commit v8 on v7

--- a/solution.py
+++ b/solution.py
@@ -19,8 +19,8 @@
     return lax.dot_general(a, b, dims, preferred_element_type=F32)
 
 
-def kernel(wave, lops, rops, pat, sizes, out1, out2, *scratch):
-    wbuf, lf, rf, rsel, lsel, va, vb, mid, f2, obuf, lsem, ssem, rsem, relay = scratch[: -2 * N_STAGE]
+def kernel(wave, lops, rops, pattern, sector, out1, obuf, *scratch):
+    wbuf, lf, rf, rsel, lsel, va, vb, mid, f2, pat, sizes, lsem, ssem, rsem, relay = scratch[: -2 * N_STAGE]
     stage1, stage2 = scratch[-2 * N_STAGE : -N_STAGE], scratch[-N_STAGE:]
     ops, sec = lax.axis_index("ops"), lax.axis_index("sec")
     x, zh, c = ops // 8, (ops // 2) % 4, ops % 2
@@ -74,7 +74,11 @@
     load_w = pltpu.make_async_copy(wave, wbuf, lsem.at[0])
     load_r = pltpu.make_async_copy(rops, rf, lsem.at[1])
     load_l = pltpu.make_async_copy(lops, lf, lsem.at[2])
+    load_s = pltpu.make_async_copy(sector, sizes, lsem.at[3])
+    load_p = pltpu.make_async_copy(pattern, pat, lsem.at[4])
     load_w.start()
+    load_s.start()
+    load_p.start()
     load_r.start()
     load_l.start()
     partners = [other] + [to_y(d) for d in (1, 2, 3)] + [to_x(d) for d in (1, 2, 3)] + [to_z(d) for d in (1, 2, -2, -1)]
@@ -83,6 +87,7 @@
         pl.semaphore_signal(barrier, inc=1, device_id=device, device_id_type=MESH)
 
     load_w.wait()
+    load_s.wait()
     row = lax.broadcasted_iota(jnp.int32, (16, 512), 0) + (zl * 128 + y * 32)
     col = lax.broadcasted_iota(jnp.int32, (16, 512), 1)
 
@@ -268,6 +273,7 @@
     start = gather(va, None, True)
     next(start)
     next(start)
+    load_p.wait()
     load_r.wait()
     load_l.wait()
     pick_t = pick((128, 512), 1)
@@ -339,16 +345,8 @@
         right_part(c, ch)
         next(flows[ch])
         right_part(1 - c, ch)
-    stores = []
-
-    def store(src, dst, index):
-        for rh in range(2):
-            for bp in range(2):
-                cp = pltpu.make_async_copy(src.at[:, :, rh, bp], dst.at[:, :, bp, rh], lsem.at[index + 2 * rh + bp])
-                cp.start()
-                stores.append(cp)
-
-    store(vb.at[zl], out1, 5)
+    store = pltpu.make_async_copy(vb.at[zl], out1, lsem.at[5])
+    store.start()
 
     def pair2(cc, xx):
         cols = []
@@ -385,26 +383,21 @@
     run(flows, 2)
     drain()
     run(flows, 4)
-    store(obuf, out2, 11)
     drain()
-    for cp in stores:
-        cp.wait()
+    store.wait()
     assert count[0] == N_ARRIVALS, count
 
 
-def hand_over(first, second, out1, out2, held, sem):
+def hand_over(first, second, out1, out2, sem):
     steps = []
     for i, (src, dst) in enumerate(((first, out1), (second, out2))):
-        for k in range(4):
-            part = pl.ds(4 * k, 4)
-            load = pltpu.make_async_copy(src.at[part], held.at[i, part], sem.at[i, k, 0])
-            load.start()
-            steps.append((load, pltpu.make_async_copy(held.at[i, part], dst.at[part], sem.at[i, k, 1])))
-    for load, store in steps:
-        load.wait()
-        store.start()
-    for _, store in steps:
-        store.wait()
+        for rh in range(2):
+            for bp in range(2):
+                steps.append(pltpu.make_async_copy(src.at[:, :, rh, bp], dst.at[:, :, bp, rh], sem.at[i, rh, bp]))
+    for step in steps:
+        step.start()
+    for step in steps:
+        step.wait()
 
 
 def on_device(wave_t, left_ops, right_ops, pattern, sector_size):
@@ -427,13 +420,14 @@
         ]
 
     hbm = pl.BlockSpec(memory_space=pl.ANY)
-    smem = pl.BlockSpec(memory_space=pltpu.SMEM)
-    out = jax.ShapeDtypeStruct((2, 4, 2, 2, 16, 512), BF)
+    vmem = pl.BlockSpec(memory_space=pltpu.VMEM)
+    shape = (2, 4, 2, 2, 16, 512)
+    operands = [wave_t.reshape(shape), left_ops, right_ops, pattern, sector_size]
     first, second = pl.pallas_call(
         kernel,
-        out_shape=(out, out),
-        in_specs=[hbm, hbm, hbm, smem, smem],
-        out_specs=(hbm, hbm),
+        out_shape=(pltpu.VMEM(shape, BF), pltpu.VMEM(shape, BF)),
+        in_specs=[hbm] * 5,
+        out_specs=(vmem, vmem),
         scratch_shapes=[
             pltpu.VMEM((2, 4, 2, 2, 16, 512), BF),
             pltpu.VMEM((3, 512, 512), BF),
@@ -444,8 +438,9 @@
             pltpu.VMEM((4, 2, 4, 2, 2, 16, 512), BF),
             pltpu.VMEM((3, 16, 4, 2, 16, 128), BF),
             pltpu.VMEM((2, 2, 4, 16, 128), BF),
-            pltpu.VMEM((2, 4, 2, 2, 16, 512), BF),
-            pltpu.SemaphoreType.DMA((16,)),
+            pltpu.SMEM((3, 16), jnp.int32),
+            pltpu.SMEM((16,), jnp.int32),
+            pltpu.SemaphoreType.DMA((6,)),
             pltpu.SemaphoreType.DMA((N_SENDS,)),
             pltpu.SemaphoreType.DMA((N_ARRIVALS,)),
             pltpu.SemaphoreType.REGULAR((1,)),
@@ -453,20 +448,20 @@
             *stage(64, 128),
         ],
         compiler_params=pltpu.CompilerParams(
-            collective_id=0, has_side_effects=True, vmem_limit_bytes=58 * 2**20
+            collective_id=0, has_side_effects=True, vmem_limit_bytes=40 * 2**20
         ),
         name="hamiltonian",
-    )(wave_t.reshape(2, 4, 2, 2, 16, 512), left_ops, right_ops, pattern, sector_size)
-    result = jax.ShapeDtypeStruct((16, 32, 512), BF)
-    return pl.pallas_call(
+    )(*[pltpu.with_memory_space_constraint(a, pltpu.HBM) for a in operands])
+    result = jax.ShapeDtypeStruct(shape, BF)
+    first, second = pl.pallas_call(
         hand_over,
         out_shape=(result, result),
-        in_specs=[hbm, hbm],
+        in_specs=[vmem, vmem],
         out_specs=(hbm, hbm),
-        scratch_shapes=[pltpu.VMEM((2, 16, 32, 512), BF), pltpu.SemaphoreType.DMA((2, 4, 2))],
-        compiler_params=pltpu.CompilerParams(vmem_limit_bytes=58 * 2**20),
+        scratch_shapes=[pltpu.SemaphoreType.DMA((2, 2, 2))],
         name="hand_over",
-    )(first.reshape(16, 32, 512), second.reshape(16, 32, 512))
+    )(*[pltpu.with_memory_space_constraint(a, pltpu.VMEM) for a in (first, second)])
+    return first.reshape(16, 32, 512), second.reshape(16, 32, 512)
 
 
 def solution(mesh):

time: 99.2 us -> 96.3 us (0.971)
  Pallas kernels: 98.4 us -> 95.5 us
    pallas_call x2, Pallas kernels: 98.4 us -> 95.5 us  [the longest x1 94.5 us: on_device(): pl.pallas_call(kernel, out_shape=(pltpu.VMEM(shape, BF), pltpu.VMEM(shape...]
where the time goes in v8:
time: 96.3 us; the launch traced here: 96.1 us
  Pallas kernels  95.5 us (99%)
    pallas_call x1, Pallas kernels, on_device(): pl.pallas_call(kernel, out_shape=(pltpu.VMEM(shape, BF), pltpu.VMEM(shape...  94.5 us

profile of v8, /device:TPU:1, one launch (start us, length us, event | category | flops | bytes accessed | tf_op | source)
XLA Modules:
  0.0 96.1 jit_solution(17214609299868180881)
XLA Ops:
  0.6 94.5 %hamiltonian.1 = (bf16[2,4,2,2,16,512]{5,4,3,2,1,0:T(8,128)(2,1)S(1)}, bf16[2,4,2,2,16,512]{5,4,3,2,1,0:T(8,128)(2,1)S(1)}) custom-call(bf16[2,4,2,2,16,512]{5,4,3,2,1,0:T(8,128)(2,1)} %bitcast.3, bf16[3,512,512]{2,1,0:T(8,128)(2,1)} %lops.1, bf16[3,512,512]{2,1,0:T(8,128)(2,1)} %rops.1, s32[3,16]{1,0:T(4,128)} %pattern.1, s32[16]{0:T(128)} %sector.1), custom_call_target="tpu_custom_call" | custom-call | tf_op jit(solution)/shard_map/hamiltonian/pallas_call | solution.py:426
  95.1 1.0 %hand_over.1 = (bf16[2,4,2,2,16,512]{5,4,3,2,1,0:T(8,128)(2,1)}, bf16[2,4,2,2,16,512]{5,4,3,2,1,0:T(8,128)(2,1)}) custom-call(bf16[2,4,2,2,16,512]{5,4,3,2,1,0:T(8,128)(2,1)S(1)} %get-tuple-element.6.first, bf16[2,4,2,2,16,512]{5,4,3,2,1,0:T(8,128)(2,1)S(1)} %get-tuple-element.7.second), custom_call_target="tpu_custom_call" | custom-call | tf_op jit(solution)/shard_map/hand_over/pallas_call | solution.py:456

commit v9 on v8

--- a/solution.py
+++ b/solution.py
@@ -116,10 +116,11 @@
 
         def z_send(xx, bp, i0):
             block = v.at[zl, c, xx, rows, bp]
-            group = [(block, block, i0, to_z(1)), (block, block, i0 + 1, to_z(-1))]
+            group = []
             for rh in halves:
                 part = v.at[zl, c, xx, rh, bp]
                 group.append((part, part, i0 + 2 + rh, to_z(2 - 4 * rh)))
+            group += [(block, block, i0, to_z(1)), (block, block, i0 + 1, to_z(-1))]
             send_all(group, v.at[zl, c, pl.ds(0, 3), rows, bp])
 
         def z_arrived(xx, bp, k, i0):
@@ -131,7 +132,7 @@
 
         def x_send(zz, bp, indices):
             block = v.at[zz, c, x, rows, bp]
-            group = [(block, block, i, to_x(d)) for d, i in zip((1, 2, 3), indices)]
+            group = [(block, block, i, to_x(d)) for d, i in zip((2, 1, 3), (indices[1], indices[0], indices[2]))]
             send_all(group, v.at[zz, c, pl.ds(0, 3), rows, bp])
 
         z_send(x, 0, a1)
@@ -193,7 +194,7 @@
             if k % 2:
                 two = pl.ds(k - 1, 2)
                 group = [
-                    (s0.at[two, ch, 0, (y + e) % 4], r1y.at[ch, e - 1, two], py + 2 * ch + k // 2, to_y(e)) for e in (1, 2, 3)
+                    (s0.at[two, ch, 0, (y + e) % 4], r1y.at[ch, e - 1, two], py + 2 * ch + k // 2, to_y(e)) for e in (2, 1, 3)
                 ]
                 send_all(group, r1y.at[ch, :, two])
 
@@ -228,7 +229,7 @@
                 if k < 3:
                     t1[ch, k] = sum_t1(k).astype(BF)
                     if k == 2:
-                        group = [(t1.at[ch, m], r2x.at[ch, m], qx + ch, to_x(m + 1)) for m in range(3)]
+                        group = [(t1.at[ch, m], r2x.at[ch, m], qx + ch, to_x(m + 1)) for m in (1, 0, 2)]
                         send_all(group, r2x.at[ch])
             arrived(r1x.at[ch], px + ch)
             mine = s0[3, ch, 1].astype(F32)
@@ -238,7 +239,7 @@
             for e in (1, 2, 3):
                 q = (y + e) % 4
                 t2b[ch, e - 1] = t2[ch, q].astype(BF)
-            group = [(t2b.at[ch, e - 1], r2y.at[ch, e - 1], qy + ch, to_y(e)) for e in (1, 2, 3)]
+            group = [(t2b.at[ch, e - 1], r2y.at[ch, e - 1], qy + ch, to_y(e)) for e in (2, 1, 3)]
             send_all(group, r2y.at[ch])
             yield
             w0 = sum_t1(3)
@@ -368,8 +369,8 @@
         here = obuf.at[c, x, ch, :, :, lanes(zl)]
         g2, gc = copies(1), copies(1)
         pltpu.make_async_copy(f2.at[ch, :, zl], here, rsem.at[g2]).start()
-        for d in (0, 1, -1, 2 - 4 * ch):
-            group = [(f2.at[ch, :, (zl + d + 4) % 4], here, g2, to_xz(dx, d)) for dx in (0, 1, 3, 2) if d or dx]
+        for d in (2 - 4 * ch, 1, -1, 0):
+            group = [(f2.at[ch, :, (zl + d + 4) % 4], here, g2, to_xz(dx, d)) for dx in (2, 1, 3, 0) if d or dx]
             send_all(group, f2.at[ch, :, pl.ds(0, len(group))])
         yield
         block = obuf.at[c, :, ch]

time: 96.3 us -> 95.7 us (level)
  no operation moved by 1% of the time
where the time goes in v9:
time: 95.7 us; the launch traced here: 95.5 us
  Pallas kernels  94.9 us (99%)
    pallas_call x1, Pallas kernels, on_device(): pl.pallas_call(kernel, out_shape=(pltpu.VMEM(shape, BF), pltpu.VMEM(shape...  93.9 us

profile of v9, /device:TPU:1, one launch (start us, length us, event | category | flops | bytes accessed | tf_op | source)
XLA Modules:
  0.0 95.5 jit_solution(11298391842901403165)
XLA Ops:
  0.6 93.9 %hamiltonian.1 = (bf16[2,4,2,2,16,512]{5,4,3,2,1,0:T(8,128)(2,1)S(1)}, bf16[2,4,2,2,16,512]{5,4,3,2,1,0:T(8,128)(2,1)S(1)}) custom-call(bf16[2,4,2,2,16,512]{5,4,3,2,1,0:T(8,128)(2,1)} %bitcast.3, bf16[3,512,512]{2,1,0:T(8,128)(2,1)} %lops.1, bf16[3,512,512]{2,1,0:T(8,128)(2,1)} %rops.1, s32[3,16]{1,0:T(4,128)} %pattern.1, s32[16]{0:T(128)} %sector.1), custom_call_target="tpu_custom_call" | custom-call | tf_op jit(solution)/shard_map/hamiltonian/pallas_call | solution.py:427
  94.5 1.0 %hand_over.1 = (bf16[2,4,2,2,16,512]{5,4,3,2,1,0:T(8,128)(2,1)}, bf16[2,4,2,2,16,512]{5,4,3,2,1,0:T(8,128)(2,1)}) custom-call(bf16[2,4,2,2,16,512]{5,4,3,2,1,0:T(8,128)(2,1)S(1)} %get-tuple-element.6.first, bf16[2,4,2,2,16,512]{5,4,3,2,1,0:T(8,128)(2,1)S(1)} %get-tuple-element.7.second), custom_call_target="tpu_custom_call" | custom-call | tf_op jit(solution)/shard_map/hand_over/pallas_call | solution.py:457
